TPU v7x, 512 devices: a whole 4x8x8 slice. The times are simulated.
512 devices in a mesh: head: 8 (over y_hi, x), ctx: 64 (over z, y_lo, core).
Axes of the slice: x: 4, y: 8 (y_hi: 2, y_lo: 4; y = y_hi * 4 + y_lo), z: 8, core: 2. Of those that a mesh axis runs over, the one named last changes fastest.
Arguments:
- queries: bfloat16 [32768, 8192], P(('head', 'ctx')), may hold values from -4.5 to 4.5
- key_tensor: bfloat16 [32768, 1024], P(('head', 'ctx')), may hold values from -4.5 to 4.5
- value_tensor: bfloat16 [32768, 1024], P(('head', 'ctx')), may hold values from -6 to 6
- positions: int32 [32768], P(('head', 'ctx')), may hold values from 0 to 32767, as said below
Outputs:
- attended: bfloat16 [32768, 8192], P(('head', 'ctx'))
Inputs may be any that keep to these rules, and one draw needn't show every extreme that they name: A permutation of the positions. Take the rows held by one index c of ctx, in the order of the head indices: they are two whole blocks of 256 consecutive positions in increasing order, block k and block 127 - k for some k, in either order.
All inputs are finite; a program needn't handle non-finite values.
Results may differ from a plain program's by a relative error of at most 0.0045.
Values may be sent and summed in bfloat16 or wider, within the bound.
No kernel may reach another device: no remote copies, remote signals or barrier semaphores. Data moves between devices by JAX's collectives and lax.ppermute only.
A program may use at most 64 MiB of HBM per device.

v0:
```python
import math

import jax
import jax.numpy as jnp
from jax import lax
from jax.sharding import PartitionSpec as P

HEAD_DIMENSION = 128
WINDOW_BLOCKS = 3


neg_big = -1e30


def shifted(block, axis, distance):
    devices = range(lax.axis_size(axis))
    route = [((i - distance) % len(devices), i) for i in devices]
    return lax.ppermute(block, axis, route)


def attend(carried, q_part, q_pos, key_row_block, value_row_block, key_pos, score_scale):
    running_max, denominator, numerator = carried
    scores = (
        jnp.einsum("skgd,tkd->skgt", q_part, key_row_block, preferred_element_type=jnp.float32)
        * score_scale
    )
    visible = (key_pos[None, :] <= q_pos[:, None])[:, None, None, :]
    scores = jnp.where(visible, scores, neg_big)
    new_max = jnp.maximum(running_max, jnp.max(scores, axis=-1))
    weights = jnp.where(visible, jnp.exp(scores - new_max[..., None]), 0.0)
    rescale = jnp.exp(running_max - new_max)
    denominator = denominator * rescale + jnp.sum(weights, axis=-1)
    numerator = numerator * rescale[..., None] + jnp.einsum(
        "skgt,tkd->skgd",
        weights.astype(jnp.bfloat16),
        value_row_block,
        preferred_element_type=jnp.float32,
    )
    return (new_max, denominator, numerator)


def attend_tiles(carried, q_part, q_pos, key_row_block, value_row_block, key_pos, score_scale):
    half_k = key_row_block.shape[0] // 2
    state = carried
    for k_index in range(2):
        k_lo = k_index * half_k
        state = attend(
            state,
            q_part,
            q_pos,
            key_row_block[k_lo : k_lo + half_k],
            value_row_block[k_lo : k_lo + half_k],
            key_pos[k_lo : k_lo + half_k],
            score_scale,
        )
    return state


def body(queries, key_tensor, value_tensor, positions):
    q_local, k_local, v_local = (
        lax.all_to_all(queries, "head", split_axis=1, concat_axis=0, tiled=True),
        lax.all_to_all(key_tensor, "head", split_axis=1, concat_axis=0, tiled=True),
        lax.all_to_all(value_tensor, "head", split_axis=1, concat_axis=0, tiled=True),
    )
    seq_rows = k_local.shape[0]
    kv_heads = k_local.shape[1] // HEAD_DIMENSION
    q_heads = q_local.shape[1] // HEAD_DIMENSION
    query_groups = q_heads // kv_heads
    stacked = jnp.stack(
        [
            k_local.reshape(seq_rows, kv_heads, HEAD_DIMENSION),
            v_local.reshape(seq_rows, kv_heads, HEAD_DIMENSION),
        ]
    )
    q_blocks = q_local.reshape(seq_rows, kv_heads, query_groups, HEAD_DIMENSION)
    q_pos = lax.all_gather(positions, "head", axis=0, tiled=True)
    score_scale = 1.0 / math.sqrt(HEAD_DIMENSION)
    initial = (
        jnp.full((seq_rows, kv_heads, query_groups), neg_big, jnp.float32),
        jnp.zeros((seq_rows, kv_heads, query_groups), jnp.float32),
        jnp.zeros((seq_rows, kv_heads, query_groups, HEAD_DIMENSION), jnp.float32),
    )
    carried = attend_tiles(initial, q_blocks, q_pos, stacked[0], stacked[1], q_pos, score_scale)
    moving = stacked
    moving_pos = q_pos
    for cycle_step in range(1, WINDOW_BLOCKS + 1):
        moving = shifted(moving, "ctx", 1)
        moving_pos = shifted(moving_pos, "ctx", 1)
        carried = attend_tiles(
            carried, q_blocks, q_pos, moving[0], moving[1], moving_pos, score_scale
        )
    running_max, denominator, numerator = carried
    result = (
        (numerator / denominator[..., None])
        .astype(jnp.bfloat16)
        .reshape(seq_rows, q_heads * HEAD_DIMENSION)
    )
    return lax.all_to_all(result, "head", split_axis=0, concat_axis=1, tiled=True)


def solution(mesh):
    return jax.shard_map(
        body,
        mesh=mesh,
        in_specs=(
            P(("head", "ctx"), None),
            P(("head", "ctx"), None),
            P(("head", "ctx"), None),
            P(("head", "ctx")),
        ),
        out_specs=P(("head", "ctx"), None),
        check_vma=False,
    )
```

profile of v0, /device:TPU:2, one launch (start us, length us, event | category | flops | bytes accessed | tf_op | source)
XLA Modules:
  0.0 176.0 jit_solution(6381692488964491285)
XLA Ops:
  1.6 10.1 %all-to-all-start = ((bf16[64,8,128]{2,0,1:T(8,128)(2,1)}), bf16[64,8,128]{2,0,1:T(8,128)(2,1)S(1)}, u32[]{:S(2)}, u32[]{:S(2)}) async-start(bf16[64,8,128]{2,0,1:T(8,128)(2,1)} %copy_bitcast_fusion.2), calls=%async_computation | async-start | bytes 262144 | tf_op jit(solution)/shard_map/all_to_all | solution.py:62
  11.7 1.6 copy_bitcast_fusion.1
  13.2 7.4 %all-to-all-done = bf16[64,8,128]{2,0,1:T(8,128)(2,1)S(1)} async-done(((bf16[64,8,128]{2,0,1:T(8,128)(2,1)}), bf16[64,8,128]{2,0,1:T(8,128)(2,1)S(1)}, u32[]{:S(2)}, u32[]{:S(2)}) %all-to-all-start) | async-done | bytes 131104 | tf_op jit(solution)/shard_map/all_to_all | solution.py:62
  20.7 4.8 %all-to-all-start.2 = ((bf16[64,8,128]{2,0,1:T(8,128)(2,1)}), bf16[64,8,128]{2,0,1:T(8,128)(2,1)S(1)}, u32[]{:S(2)}, u32[]{:S(2)}) async-start(bf16[64,8,128]{2,0,1:T(8,128)(2,1)} %copy_bitcast_fusion.1), calls=%async_computation.2 | async-start | bytes 262144 | tf_op jit(solution)/shard_map/all_to_all | solution.py:63
  25.4 2.3 %copy.158 = bf16[8,8,8,1024]{3,2,0,1:T(8,128)(2,1)} copy(bf16[8,8,8,1024]{3,2,1,0:T(8,128)(2,1)} %bitcast.350) | data formatting | bytes 2097152 | tf_op jit(solution)/shard_map/all_to_all | solution.py:61
  27.7 6.7 %all-to-all-done.2 = bf16[64,8,128]{2,0,1:T(8,128)(2,1)S(1)} async-done(((bf16[64,8,128]{2,0,1:T(8,128)(2,1)}), bf16[64,8,128]{2,0,1:T(8,128)(2,1)S(1)}, u32[]{:S(2)}, u32[]{:S(2)}) %all-to-all-start.2) | async-done | bytes 131104 | tf_op jit(solution)/shard_map/all_to_all | solution.py:63
  34.5 5.0 %all-to-all-start.1 = ((bf16[64,8,1024]{2,0,1:T(8,128)(2,1)}), bf16[64,8,1024]{2,0,1:T(8,128)(2,1)S(1)}, u32[]{:S(2)}, u32[]{:S(2)}) async-start(bf16[64,8,1024]{2,0,1:T(8,128)(2,1)} %bitcast.335), calls=%async_computation.1 | async-start | bytes 2097152 | tf_op jit(solution)/shard_map/all_to_all | solution.py:61
  41.7 18.9 %all-reduce = s32[512]{0:T(512)S(1)} all-reduce(s32[512]{0:T(512)S(1)} %dynamic-update-slice), channel_id=1, replica_groups=mesh['head'=8,'ctx'=64] {'head'}, use_global_device_ids=true, to_apply=%add | all-reduce | flops 512 | bytes 4096
  60.7 1.9 %collective-permute-start = (s32[512]{0:T(512)S(1)}, s32[512]{0:T(512)S(1)}, u32[]{:S(2)}, u32[]{:S(2)}) collective-permute-start(s32[512]{0:T(512)S(1)} %all-reduce), channel_id=1, source_target_pairs={{63,0},{0,1},{1,2},{2,3},{3,4},{4,5},{5,6},{6,7},{7,8},{8,9},{9,10... | collective-permute-start | bytes 6152 | tf_op jit(solution)/shard_map/ppermute | solution.py:18
  62.6 7.0 %collective-permute-done = s32[512]{0:T(512)S(1)} collective-permute-done((s32[512]{0:T(512)S(1)}, s32[512]{0:T(512)S(1)}, u32[]{:S(2)}, u32[]{:S(2)}) %collective-permute-start) | collective-permute-done | bytes 2080 | tf_op jit(solution)/shard_map/ppermute | solution.py:18
  69.6 1.9 %collective-permute-start.2 = (s32[512]{0:T(512)S(1)}, s32[512]{0:T(512)S(1)}, u32[]{:S(2)}, u32[]{:S(2)}) collective-permute-start(s32[512]{0:T(512)S(1)} %collective-permute-done), channel_id=1, source_target_pairs={{63,0},{0,1},{1,2},{2,3},{3,4},{4,5},{5,6},{6,7},{7,8},{8,9},{9,10... | collective-permute-start | bytes 6152 | tf_op jit(solution)/shard_map/ppermute | solution.py:18
  71.5 9.4 %collective-permute-done.2 = s32[512]{0:T(512)S(1)} collective-permute-done((s32[512]{0:T(512)S(1)}, s32[512]{0:T(512)S(1)}, u32[]{:S(2)}, u32[]{:S(2)}) %collective-permute-start.2) | collective-permute-done | bytes 2080 | tf_op jit(solution)/shard_map/ppermute | solution.py:18
  80.9 1.9 %collective-permute-start.4 = (s32[512]{0:T(512)S(1)}, s32[512]{0:T(512)S(1)}, u32[]{:S(2)}, u32[]{:S(2)}) collective-permute-start(s32[512]{0:T(512)S(1)} %collective-permute-done.2), channel_id=1, source_target_pairs={{63,0},{0,1},{1,2},{2,3},{3,4},{4,5},{5,6},{6,7},{7,8},{8,9},{9,10... | collective-permute-start | bytes 6152 | tf_op jit(solution)/shard_map/ppermute | solution.py:18
  82.8 6.9 %collective-permute-done.4 = s32[512]{0:T(512)S(1)} collective-permute-done((s32[512]{0:T(512)S(1)}, s32[512]{0:T(512)S(1)}, u32[]{:S(2)}, u32[]{:S(2)}) %collective-permute-start.4) | collective-permute-done | bytes 2080 | tf_op jit(solution)/shard_map/ppermute | solution.py:18
  89.7 1.9 %collective-permute-start.1 = (bf16[2,512,1,128]{3,1,2,0:T(8,128)(2,1)S(1)}, bf16[2,512,1,128]{3,1,2,0:T(8,128)(2,1)S(1)}, u32[]{:S(2)}, u32[]{:S(2)}) collective-permute-start(bf16[2,512,1,128]{3,1,2,0:T(8,128)(2,1)S(1)} %pad_maximum_fusion), channel_id=1, source_target_pairs={{63,0},{0,1},{1,2},{2,3},{3,4},{4,5},{5,6},{6,7},{7,8},{8,9},{9,10... | collective-permute-start | bytes 786440 | tf_op jit(solution)/shard_map/ppermute | solution.py:18
  92.4 8.9 %collective-permute-done.1 = bf16[2,512,1,128]{3,1,2,0:T(8,128)(2,1)S(1)} collective-permute-done((bf16[2,512,1,128]{3,1,2,0:T(8,128)(2,1)S(1)}, bf16[2,512,1,128]{3,1,2,0:T(8,128)(2,1)S(1)}, u32[]{:S(2)}, u32[]{:S(2)}) %collective-permute-start.1) | collective-permute-done | bytes 262176 | tf_op jit(solution)/shard_map/ppermute | solution.py:18
  101.3 1.9 %collective-permute-start.3 = (bf16[2,512,1,128]{3,1,2,0:T(8,128)(2,1)S(1)}, bf16[2,512,1,128]{3,1,2,0:T(8,128)(2,1)S(1)}, u32[]{:S(2)}, u32[]{:S(2)}) collective-permute-start(bf16[2,512,1,128]{3,1,2,0:T(8,128)(2,1)S(1)} %collective-permute-done.1), channel_id=1, source_target_pairs={{63,0},{0,1},{1,2},{2,3},{3,4},{4,5},{5,6},{6,7},{7,8},{8,9},{9,10... | collective-permute-start | bytes 786440 | tf_op jit(solution)/shard_map/ppermute | solution.py:18
  103.3 9.6 %collective-permute-done.3 = bf16[2,512,1,128]{3,1,2,0:T(8,128)(2,1)S(1)} collective-permute-done((bf16[2,512,1,128]{3,1,2,0:T(8,128)(2,1)S(1)}, bf16[2,512,1,128]{3,1,2,0:T(8,128)(2,1)S(1)}, u32[]{:S(2)}, u32[]{:S(2)}) %collective-permute-start.3) | collective-permute-done | bytes 262176 | tf_op jit(solution)/shard_map/ppermute | solution.py:18
  112.9 1.9 %collective-permute-start.5 = (bf16[2,512,1,128]{3,1,2,0:T(8,128)(2,1)S(1)}, bf16[2,512,1,128]{3,1,2,0:T(8,128)(2,1)S(1)}, u32[]{:S(2)}, u32[]{:S(2)}) collective-permute-start(bf16[2,512,1,128]{3,1,2,0:T(8,128)(2,1)S(1)} %collective-permute-done.3), channel_id=1, source_target_pairs={{63,0},{0,1},{1,2},{2,3},{3,4},{4,5},{5,6},{6,7},{7,8},{8,9},{9,10... | collective-permute-start | bytes 786440 | tf_op jit(solution)/shard_map/ppermute | solution.py:18
  120.7 3.8 %collective-permute-done.5 = bf16[2,512,1,128]{3,1,2,0:T(8,128)(2,1)S(1)} collective-permute-done((bf16[2,512,1,128]{3,1,2,0:T(8,128)(2,1)S(1)}, bf16[2,512,1,128]{3,1,2,0:T(8,128)(2,1)S(1)}, u32[]{:S(2)}, u32[]{:S(2)}) %collective-permute-start.5) | collective-permute-done | bytes 262176 | tf_op jit(solution)/shard_map/ppermute | solution.py:18
  126.4 1.6 fusion.46
  128.0 2.3 %fusion.8 = (f32[512,8]{0,1:T(8,128)S(1)}, f32[512,8]{0,1:T(8,128)S(1)}) fusion(f32[256,512,8]{1,0,2:T(8,128)S(1)} %get-tuple-element.57, f32[512,8]{0,1:T(8,128)S(1)} %get-tuple-element.25, pred[512,256]{0,1:T(8,128)(4,1)S(1)} %get-tuple-element.26, f32[512,8]{0,1:T(8,128)S(1)} %get-tuple-element.19, f32[256,512,8]{1,0,2:T(8,128)S(1)} %get-tuple-element.55, ...), kind=kLoop, calls=%fused_computation.24 | loop fusion | flops 10477568 | bytes 8716288 | tf_op jit(solution)/shard_map/reduce_sum | solution.py:32
  130.2 1.6 fusion.43
  131.8 2.1 %fusion.20 = (f32[512,8]{0,1:T(8,128)S(1)}, f32[512,8]{0,1:T(8,128)S(1)}) fusion(f32[256,512,8]{1,0,2:T(8,128)S(1)} %get-tuple-element.45, f32[512,8]{0,1:T(8,128)S(1)} %get-tuple-element.14, pred[512,256]{0,1:T(8,128)(4,1)S(1)} %get-tuple-element.32, f32[512,8]{0,1:T(8,128)S(1)} %get-tuple-element.13, f32[256,512,8]{1,0,2:T(8,128)S(1)} %get-tuple-element.43, ...), kind=kLoop, calls=%fused_computation.36 | loop fusion | flops 10477568 | bytes 8716288 | tf_op jit(solution)/shard_map/reduce_sum | solution.py:32
  133.9 2.1 %fusion.16 = (f32[512,8]{0,1:T(8,128)S(1)}, f32[512,8]{0,1:T(8,128)S(1)}) fusion(f32[256,512,8]{1,0,2:T(8,128)S(1)} %get-tuple-element.49, f32[512,8]{0,1:T(8,128)S(1)} %get-tuple-element.16, pred[512,256]{0,1:T(8,128)(4,1)S(1)} %get-tuple-element.30, f32[512,8]{0,1:T(8,128)S(1)} %get-tuple-element.15, f32[256,512,8]{1,0,2:T(8,128)S(1)} %get-tuple-element.47, ...), kind=kLoop, calls=%fused_computation.32 | loop fusion | flops 10477568 | bytes 8716288 | tf_op jit(solution)/shard_map/reduce_sum | solution.py:32
  136.0 2.1 %fusion.12 = (f32[512,8]{0,1:T(8,128)S(1)}, f32[512,8]{0,1:T(8,128)S(1)}) fusion(f32[256,512,8]{1,0,2:T(8,128)S(1)} %get-tuple-element.53, f32[512,8]{0,1:T(8,128)S(1)} %get-tuple-element.18, pred[512,256]{0,1:T(8,128)(4,1)S(1)} %get-tuple-element.28, f32[512,8]{0,1:T(8,128)S(1)} %get-tuple-element.17, f32[256,512,8]{1,0,2:T(8,128)S(1)} %get-tuple-element.51, ...), kind=kLoop, calls=%fused_computation.28 | loop fusion | flops 10477568 | bytes 8716288 | tf_op jit(solution)/shard_map/reduce_sum | solution.py:32
  139.5 1.4 fusion.31
  140.9 1.4 fusion.34
  142.3 1.4 fusion.37
  143.7 1.4 fusion.40
  145.1 6.3 %bitcast_convert_fusion = bf16[512,1,8,128]{3,0,2,1:T(8,128)(2,1)S(1)} fusion(f32[128,512,8]{0,1,2:T(8,128)S(1)} %fusion.28, f32[128,512,8]{0,1,2:T(8,128)S(1)} %fusion.31, f32[128,512,8]{0,1,2:T(8,128)S(1)} %fusion.34, f32[128,512,8]{0,1,2:T(8,128)S(1)} %fusion.37, f32[128,512,8]{0,1,2:T(8,128)S(1)} %fusion.40, f32[512,8,128]{2,0,1:T(8,128)S(1)} %fusion.43, ...), kind=kOutput, calls=%fused_computation.72 | convolution fusion | flops 282591232 | bytes 20283392 | tf_op jit(solution)/shard_map/skgt,tkd->skgd/dot_general | solution.py:33
  152.7 22.3 %all_to_all.67 = bf16[8,64,1024]{2,1,0:T(8,128)(2,1)S(1)} all-to-all(bf16[8,64,1024]{2,1,0:T(8,128)(2,1)S(1)} %all_to_all.59), channel_id=1, replica_groups=mesh['head'=8,'ctx'=64] {'head'}, dimensions={0} | all-to-all | bytes 2097152 | tf_op jit(solution)/shard_map/all_to_all | solution.py:98
  (32 shorter events, 15.4 us)
Async XLA Ops:
  0.0 0.9 copy-start
  0.9 40.6 %copy-start.1 = (s32[64]{0:T(128)S(1)}, s32[64]{0:T(128)}, u32[]{:S(2)}) copy-start(s32[64]{0:T(128)} %param.7) | copy-start | bytes 772
  1.6 19.1 %all-to-all-start = ((bf16[64,8,128]{2,0,1:T(8,128)(2,1)}), bf16[64,8,128]{2,0,1:T(8,128)(2,1)S(1)}, u32[]{:S(2)}, u32[]{:S(2)}) async-start(bf16[64,8,128]{2,0,1:T(8,128)(2,1)} %copy_bitcast_fusion.2), calls=%async_computation | async-start | bytes 262144 | tf_op jit(solution)/shard_map/all_to_all | solution.py:62
  20.7 13.8 %all-to-all-start.2 = ((bf16[64,8,128]{2,0,1:T(8,128)(2,1)}), bf16[64,8,128]{2,0,1:T(8,128)(2,1)S(1)}, u32[]{:S(2)}, u32[]{:S(2)}) async-start(bf16[64,8,128]{2,0,1:T(8,128)(2,1)} %copy_bitcast_fusion.1), calls=%async_computation.2 | async-start | bytes 262144 | tf_op jit(solution)/shard_map/all_to_all | solution.py:63
  34.5 80.4 %all-to-all-start.1 = ((bf16[64,8,1024]{2,0,1:T(8,128)(2,1)}), bf16[64,8,1024]{2,0,1:T(8,128)(2,1)S(1)}, u32[]{:S(2)}, u32[]{:S(2)}) async-start(bf16[64,8,1024]{2,0,1:T(8,128)(2,1)} %bitcast.335), calls=%async_computation.1 | async-start | bytes 2097152 | tf_op jit(solution)/shard_map/all_to_all | solution.py:61
  60.7 8.9 %collective-permute-start = (s32[512]{0:T(512)S(1)}, s32[512]{0:T(512)S(1)}, u32[]{:S(2)}, u32[]{:S(2)}) collective-permute-start(s32[512]{0:T(512)S(1)} %all-reduce), channel_id=1, source_target_pairs={{63,0},{0,1},{1,2},{2,3},{3,4},{4,5},{5,6},{6,7},{7,8},{8,9},{9,10... | collective-permute-start | bytes 6152 | tf_op jit(solution)/shard_map/ppermute | solution.py:18
  69.6 11.3 %collective-permute-start.2 = (s32[512]{0:T(512)S(1)}, s32[512]{0:T(512)S(1)}, u32[]{:S(2)}, u32[]{:S(2)}) collective-permute-start(s32[512]{0:T(512)S(1)} %collective-permute-done), channel_id=1, source_target_pairs={{63,0},{0,1},{1,2},{2,3},{3,4},{4,5},{5,6},{6,7},{7,8},{8,9},{9,10... | collective-permute-start | bytes 6152 | tf_op jit(solution)/shard_map/ppermute | solution.py:18
  80.9 8.8 %collective-permute-start.4 = (s32[512]{0:T(512)S(1)}, s32[512]{0:T(512)S(1)}, u32[]{:S(2)}, u32[]{:S(2)}) collective-permute-start(s32[512]{0:T(512)S(1)} %collective-permute-done.2), channel_id=1, source_target_pairs={{63,0},{0,1},{1,2},{2,3},{3,4},{4,5},{5,6},{6,7},{7,8},{8,9},{9,10... | collective-permute-start | bytes 6152 | tf_op jit(solution)/shard_map/ppermute | solution.py:18
  89.7 11.6 %collective-permute-start.1 = (bf16[2,512,1,128]{3,1,2,0:T(8,128)(2,1)S(1)}, bf16[2,512,1,128]{3,1,2,0:T(8,128)(2,1)S(1)}, u32[]{:S(2)}, u32[]{:S(2)}) collective-permute-start(bf16[2,512,1,128]{3,1,2,0:T(8,128)(2,1)S(1)} %pad_maximum_fusion), channel_id=1, source_target_pairs={{63,0},{0,1},{1,2},{2,3},{3,4},{4,5},{5,6},{6,7},{7,8},{8,9},{9,10... | collective-permute-start | bytes 786440 | tf_op jit(solution)/shard_map/ppermute | solution.py:18
  101.3 11.6 %collective-permute-start.3 = (bf16[2,512,1,128]{3,1,2,0:T(8,128)(2,1)S(1)}, bf16[2,512,1,128]{3,1,2,0:T(8,128)(2,1)S(1)}, u32[]{:S(2)}, u32[]{:S(2)}) collective-permute-start(bf16[2,512,1,128]{3,1,2,0:T(8,128)(2,1)S(1)} %collective-permute-done.1), channel_id=1, source_target_pairs={{63,0},{0,1},{1,2},{2,3},{3,4},{4,5},{5,6},{6,7},{7,8},{8,9},{9,10... | collective-permute-start | bytes 786440 | tf_op jit(solution)/shard_map/ppermute | solution.py:18
  112.9 11.6 %collective-permute-start.5 = (bf16[2,512,1,128]{3,1,2,0:T(8,128)(2,1)S(1)}, bf16[2,512,1,128]{3,1,2,0:T(8,128)(2,1)S(1)}, u32[]{:S(2)}, u32[]{:S(2)}) collective-permute-start(bf16[2,512,1,128]{3,1,2,0:T(8,128)(2,1)S(1)} %collective-permute-done.3), channel_id=1, source_target_pairs={{63,0},{0,1},{1,2},{2,3},{3,4},{4,5},{5,6},{6,7},{7,8},{8,9},{9,10... | collective-permute-start | bytes 786440 | tf_op jit(solution)/shard_map/ppermute | solution.py:18
where the time goes:
time: 177 us; the launch traced here: 176 us
  waiting for transfers between devices  59.7 us (34%)
  blocking collectives  41.2 us (23%)
  starting transfers between devices  31.3 us (18%)
  matrix products  23.9 us (14%)
  local copies, waits for them, and re-layouts  9.57 us (5%)
  other arithmetic  9.36 us (5%)
    ppermute x6, waiting for transfers between devices, shifted(): return lax.ppermute(block, axis, route)  45.5 us
    all_to_all x1, blocking collectives, body(): lax.all_to_all(result, 'head', split_axis=0, concat_axis=1, tiled=True)  22.3 us
    unnamed x1, blocking collectives  18.9 us
    dot_general x8, matrix products, attend(): jnp.einsum('skgt,tkd->skgd', weights.astype(jnp.bfloat16), value_row_bloc...  16.5 us
    ppermute x6, starting transfers between devices, shifted(): return lax.ppermute(block, axis, route)  11.5 us
    all_to_all x1, starting transfers between devices, body(): lax.all_to_all(key_tensor, 'head', split_axis=1, concat_axis=0, tiled=True)  10.1 us
    reduce_sum x4, other arithmetic, attend(): denominator = denominator * rescale + jnp.sum(weights, axis=-1)  8.48 us
    all_to_all x1, waiting for transfers between devices, body(): lax.all_to_all(key_tensor, 'head', split_axis=1, concat_axis=0, tiled=True)  7.41 us
  transfers between devices with their start and end apart: 9, of which 8 were waited for; matrix products, arithmetic and copies ran while one was open for 7% of the time, Pallas kernels for 0%

commit v1 on v0

v1 whole, which is shorter than its diff:
```python
import math

import jax
import jax.numpy as jnp
from jax import lax
from jax.experimental import pallas as pl
from jax.experimental.pallas import tpu as pltpu
from jax.sharding import Mesh
from jax.sharding import PartitionSpec as P

HEAD_DIMENSION = 128
RUN = 256
ROWS = 64
FLAG_ROWS = 8
GROUP = 8
SCALE = math.log2(math.e) / math.sqrt(HEAD_DIMENSION)
NEG_BIG = -1e30
AXES = ("yh", "x", "z", "yl", "c")
SIZES = (2, 4, 8, 4, 2)
MIB = 1024 * 1024


def ring_route(shift, back):
    nyh, nx, nz, nyl, nc = SIZES
    route = []
    for yh in range(nyh):
        for x in range(nx):
            for z in range(nz):
                for yl in range(nyl):
                    for c in range(nc):
                        ring = (yh * nyl + yl - shift) % (nyh * nyl)
                        chain = (z * nyl + yl - back) % (nz * nyl)
                        z2, yl2 = divmod(chain, nyl)
                        src = (((ring // nyl * nx + x) * nz + z2) * nyl + yl2) * nc + c
                        dst = (((yh * nx + x) * nz + z) * nyl + yl) * nc + c
                        route.append((src, dst))
    return route


def vmem(count):
    return [pl.BlockSpec(memory_space=pltpu.VMEM)] * count


def smem():
    return [pl.BlockSpec(memory_space=pltpu.SMEM)]


def pack_kernel(pos_ref, k_ref, v_ref, out_ref):
    run = jnp.right_shift(pos_ref[0], 8).astype(jnp.float32)
    flags = jnp.full((FLAG_ROWS, 256), run, jnp.float32).astype(jnp.bfloat16)
    for g in range(8):
        lanes = slice(g * 128, (g + 1) * 128)
        both = jnp.concatenate([k_ref[:, lanes], v_ref[:, lanes]], axis=1)
        out_ref[g] = jnp.concatenate([both, flags], axis=0)


def pack(positions, key_tensor, value_tensor):
    return pl.pallas_call(
        pack_kernel,
        out_shape=jax.ShapeDtypeStruct((8, ROWS + FLAG_ROWS, 256), jnp.bfloat16),
        in_specs=smem() + vmem(2),
        out_specs=vmem(1)[0],
        compiler_params=pltpu.CompilerParams(vmem_limit_bytes=56 * MIB),
    )(positions, key_tensor, value_tensor)


def repack_kernel(in_ref, out_ref):
    flags = []
    for c in range(2):
        for x in range(4):
            block = in_ref[c * 4 + x]
            at = c * RUN + x * ROWS
            out_ref[at : at + ROWS, :] = block[0:ROWS, :]
        flags.append(block[ROWS : ROWS + FLAG_ROWS, 0:128])
    line = jnp.concatenate(flags, axis=1)
    out_ref[2 * RUN : 2 * RUN + 16, :] = jnp.concatenate([line, line], axis=0)


def relay_kernel(own_ref, other_ref, out_ref):
    last = slice(2 * RUN, 2 * RUN + 16)
    out_ref[0:RUN, :] = own_ref[RUN : 2 * RUN, :]
    out_ref[RUN : 2 * RUN, :] = other_ref[RUN : 2 * RUN, :]
    out_ref[last, 0:128] = own_ref[last, 128:256]
    out_ref[last, 128:256] = other_ref[last, 128:256]


def rearrange(kernel, *operands):
    return pl.pallas_call(
        kernel,
        out_shape=jax.ShapeDtypeStruct((2 * RUN + 16, 256), jnp.bfloat16),
        in_specs=vmem(len(operands)),
        out_specs=vmem(1)[0],
        compiler_params=pltpu.CompilerParams(vmem_limit_bytes=4 * MIB),
    )(*operands)


def flag(ref, half):
    tile = ref[2 * RUN : 2 * RUN + 16, half * 128 : (half + 1) * 128].astype(jnp.float32)
    return jnp.max(tile).astype(jnp.int32)


def blocks(ref):
    return [(ref, 0, flag(ref, 0)), (ref, RUN, flag(ref, 1))]


def gather_visible(slots, own_run, kv_ref, start):
    count = jnp.int32(start)
    for ref, row, run in slots:
        seen = run < own_run
        at = count

        @pl.when(seen)
        def _(ref=ref, row=row, at=at):
            kv_ref[at] = ref[row : row + RUN, :]

        count = count + seen.astype(jnp.int32)
    return count


def scores_of(q_ref, i, h, keys):
    q = q_ref[i * RUN : (i + 1) * RUN, h * 128 : (h + 1) * 128]
    return lax.dot_general(q, keys, (((1,), (1,)), ((), ())), preferred_element_type=jnp.float32)


def lane_fold(s):
    return jnp.maximum(s[:, 0:128], s[:, 128:256])


def add_values(s_ref, m_ref, acc_ref, kv_ref, i, j):
    values = jnp.concatenate([kv_ref[j, :, 128:256], jnp.ones((RUN, 128), jnp.bfloat16)], axis=1)
    for h in range(GROUP):
        m = m_ref[i, h]
        s = s_ref[j, h]
        weights = jnp.concatenate(
            [jnp.exp2((s[:, 0:128] - m) * SCALE), jnp.exp2((s[:, 128:256] - m) * SCALE)], axis=1
        )
        part = jnp.dot(weights.astype(jnp.bfloat16), values, preferred_element_type=jnp.float32)
        acc_ref[i, h] = acc_ref[i, h] + part


def first_kernel(q_ref, own_ref, p1_ref, p2_ref, m_ref, acc_ref, kv_ref, s_ref):
    own, other, behind = blocks(own_ref), blocks(p1_ref), blocks(p2_ref)
    slots = [[other[0]] + behind, [other[1], own[0], other[0]] + behind]
    lower = lax.broadcasted_iota(jnp.int32, (RUN, RUN), 0) >= lax.broadcasted_iota(
        jnp.int32, (RUN, RUN), 1
    )
    for i in range(2):
        kv_ref[0] = own_ref[i * RUN : (i + 1) * RUN, :]
        count = gather_visible(slots[i], own[i][2], kv_ref, 1)
        keys = kv_ref[0, :, 0:128]
        for h in range(GROUP):
            s = jnp.where(lower, scores_of(q_ref, i, h, keys), NEG_BIG)
            s_ref[0, h] = s
            m_ref[i, h] = lane_fold(s)

        @pl.loop(1, count)
        def _(j):
            keys = kv_ref[j, :, 0:128]
            for h in range(GROUP):
                s = scores_of(q_ref, i, h, keys)
                s_ref[j, h] = s
                m_ref[i, h] = jnp.maximum(m_ref[i, h], lane_fold(s))

        for h in range(GROUP):
            m_ref[i, h] = jnp.broadcast_to(jnp.max(m_ref[i, h], axis=1, keepdims=True), (RUN, 128))
            acc_ref[i, h] = jnp.zeros((RUN, 256), jnp.float32)

        @pl.loop(0, count)
        def _(j):
            add_values(s_ref, m_ref, acc_ref, kv_ref, i, j)


def second_kernel(
    q_ref, own_ref, p3_ref, p4_ref, m1_ref, acc1_ref, out_ref, m_ref, acc_ref, kv_ref, s_ref
):
    own, behind = blocks(own_ref), blocks(p4_ref)
    slots = [behind + blocks(p3_ref), behind]
    for i in range(2):
        count = gather_visible(slots[i], own[i][2], kv_ref, 0)
        for h in range(GROUP):
            m_ref[i, h] = m1_ref[i, h]

        @pl.loop(0, count)
        def _(j):
            keys = kv_ref[j, :, 0:128]
            for h in range(GROUP):
                s = scores_of(q_ref, i, h, keys)
                s_ref[j, h] = s
                m_ref[i, h] = jnp.maximum(m_ref[i, h], lane_fold(s))

        for h in range(GROUP):
            m = jnp.broadcast_to(jnp.max(m_ref[i, h], axis=1, keepdims=True), (RUN, 128))
            m_ref[i, h] = m
            rescale = jnp.exp2((m1_ref[i, h] - m) * SCALE)
            acc_ref[i, h, :, 0:128] = acc1_ref[i, h, :, 0:128] * rescale
            acc_ref[i, h, :, 128:256] = acc1_ref[i, h, :, 128:256] * rescale

        @pl.loop(0, count)
        def _(j):
            add_values(s_ref, m_ref, acc_ref, kv_ref, i, j)

        for h in range(GROUP):
            out_ref[i * RUN : (i + 1) * RUN, h * 128 : (h + 1) * 128] = (
                acc_ref[i, h, :, 0:128] / acc_ref[i, h, :, 128:256]
            ).astype(jnp.bfloat16)


MAX_SHAPE = (2, GROUP, RUN, 128)
ACC_SHAPE = (2, GROUP, RUN, 256)


def first_part(*operands):
    return pl.pallas_call(
        first_kernel,
        out_shape=(
            jax.ShapeDtypeStruct(MAX_SHAPE, jnp.float32),
            jax.ShapeDtypeStruct(ACC_SHAPE, jnp.float32),
        ),
        in_specs=vmem(4),
        out_specs=tuple(vmem(2)),
        scratch_shapes=[
            pltpu.VMEM((6, RUN, 256), jnp.bfloat16),
            pltpu.VMEM((6, GROUP, RUN, 256), jnp.float32),
        ],
        compiler_params=pltpu.CompilerParams(vmem_limit_bytes=24 * MIB),
        cost_estimate=pl.CostEstimate(flops=8 << 29, bytes_accessed=8 << 20, transcendentals=4 << 20),
    )(*operands)


def second_part(*operands):
    return pl.pallas_call(
        second_kernel,
        out_shape=jax.ShapeDtypeStruct((2 * RUN, GROUP * 128), jnp.bfloat16),
        in_specs=vmem(6),
        out_specs=vmem(1)[0],
        scratch_shapes=[
            pltpu.VMEM(MAX_SHAPE, jnp.float32),
            pltpu.VMEM(ACC_SHAPE, jnp.float32),
            pltpu.VMEM((4, RUN, 256), jnp.bfloat16),
            pltpu.VMEM((4, GROUP, RUN, 256), jnp.float32),
        ],
        compiler_params=pltpu.CompilerParams(vmem_limit_bytes=24 * MIB),
        cost_estimate=pl.CostEstimate(flops=4 << 29, bytes_accessed=8 << 20, transcendentals=2 << 20),
    )(*operands)


def body(queries, key_tensor, value_tensor, positions):
    group = ("c", "x")
    packed = pack(positions, key_tensor, value_tensor)
    own = rearrange(
        repack_kernel, lax.all_to_all(packed, group, split_axis=0, concat_axis=0, tiled=True)
    )
    p1 = lax.ppermute(own, AXES, ring_route(4, 0))
    p2 = lax.ppermute(own, AXES, ring_route(1, 1))
    p4 = lax.ppermute(own, AXES, ring_route(5, 1))
    p3 = lax.ppermute(rearrange(relay_kernel, own, p1), AXES, ring_route(2, 2))
    q = lax.all_to_all(
        queries.reshape(ROWS, 8, GROUP * 128), group, split_axis=1, concat_axis=0, tiled=True
    ).reshape(2 * RUN, GROUP * 128)
    m1, acc1 = first_part(q, own, p1, p2)
    out = second_part(q, own, p3, p4, m1, acc1)
    result = lax.all_to_all(
        out.reshape(8, ROWS, GROUP * 128), group, split_axis=0, concat_axis=2, tiled=True
    )
    return result.reshape(ROWS, 8 * GROUP * 128)


def solution(mesh):
    finer = Mesh(mesh.devices.reshape(SIZES), AXES)
    return jax.shard_map(
        body,
        mesh=finer,
        in_specs=(P(AXES, None), P(AXES, None), P(AXES, None), P(AXES)),
        out_specs=P(AXES, None),
        check_vma=False,
    )
```

time: 177 us -> 94.3 us (0.53)
  the two profiles are of different devices: /device:TPU:2 before, /device:TPU:1 now
where the time goes in v1:
time: 94.3 us; the launch traced here: 93.8 us
  waiting for transfers between devices  30.1 us (32%)
  starting transfers between devices  24.1 us (26%)
  blocking collectives  23.8 us (25%)
  Pallas kernels  12.5 us (13%)
  local copies, waits for them, and re-layouts  3.35 us (4%)
    all_to_all x1, blocking collectives, body(): lax.all_to_all(out.reshape(8, ROWS, GROUP * 128), group, split_axis=0, co...  23.8 us
    ppermute x1, waiting for transfers between devices, body(): p1 = lax.ppermute(own, AXES, ring_route(4, 0))  11.3 us
    all_to_all x1, starting transfers between devices, body(): lax.all_to_all(packed, group, split_axis=0, concat_axis=0, tiled=True)  10.2 us
    ppermute x1, waiting for transfers between devices, body(): p2 = lax.ppermute(own, AXES, ring_route(1, 1))  8.94 us
    pallas_call x1, Pallas kernels, first_part(): pl.pallas_call(first_kernel, out_shape=(jax.ShapeDtypeStruct(MAX_SHAPE, j...  6.6 us
    ppermute x1, waiting for transfers between devices, body(): p4 = lax.ppermute(own, AXES, ring_route(5, 1))  5.21 us
    all_to_all x1, waiting for transfers between devices, body(): lax.all_to_all(packed, group, split_axis=0, concat_axis=0, tiled=True)  4.63 us
    pallas_call x1, Pallas kernels, second_part(): pl.pallas_call(second_kernel, out_shape=jax.ShapeDtypeStruct((2 * RUN, GR...  4.11 us
  transfers between devices with their start and end apart: 6, of which 4 were waited for; matrix products, arithmetic and copies ran while one was open for 2% of the time, Pallas kernels for 7%

profile of v1, /device:TPU:1, one launch (start us, length us, event | category | flops | bytes accessed | tf_op | source)
XLA Modules:
  0.0 93.8 jit_solution(11474800076485859135)
XLA Ops:
  0.0 1.7 %shard_map.46 = bf16[8,72,256]{2,1,0:T(8,128)(2,1)} custom-call(s32[64]{0:T(128)} %pos_ref.1, bf16[64,1024]{1,0:T(8,128)(2,1)} %k_ref.1, bf16[64,1024]{1,0:T(8,128)(2,1)} %v_ref.1), custom_call_target="tpu_custom_call" | custom-call | tf_op jit(solution)/shard_map/pallas_call | solution.py:58
  1.7 10.2 %all-to-all-start.1 = ((bf16[8,72,256]{2,1,0:T(8,128)(2,1)}), bf16[8,72,256]{2,1,0:T(8,128)(2,1)S(1)}, u32[]{:S(2)}, u32[]{:S(2)}) async-start(bf16[8,72,256]{2,1,0:T(8,128)(2,1)} %shard_map.46), calls=%async_computation.1 | async-start | bytes 589824 | tf_op jit(solution)/shard_map/all_to_all | solution.py:251
  12.0 2.3 %copy.11 = bf16[8,8,8,1024]{3,2,0,1:T(8,128)(2,1)} copy(bf16[8,8,8,1024]{3,2,1,0:T(8,128)(2,1)} %bitcast.22) | data formatting | bytes 2097152 | tf_op jit(solution)/shard_map/reshape | solution.py:258
  14.2 4.6 %all-to-all-done.1.in_ref = bf16[8,72,256]{2,1,0:T(8,128)(2,1)S(1)} async-done(((bf16[8,72,256]{2,1,0:T(8,128)(2,1)}), bf16[8,72,256]{2,1,0:T(8,128)(2,1)S(1)}, u32[]{:S(2)}, u32[]{:S(2)}) %all-to-all-start.1) | async-done | bytes 294944 | tf_op jit(solution)/shard_map/all_to_all | solution.py:251
  18.9 3.8 %all-to-all-start = ((bf16[64,8,1024]{2,0,1:T(8,128)(2,1)}), bf16[64,8,1024]{2,0,1:T(8,128)(2,1)S(1)}, u32[]{:S(2)}, u32[]{:S(2)}) async-start(bf16[64,8,1024]{2,0,1:T(8,128)(2,1)} %bitcast.17), calls=%async_computation | async-start | bytes 2097152 | tf_op jit(solution)/shard_map/all_to_all | solution.py:257
  22.7 3.0 %collective-permute-start = (bf16[528,256]{1,0:T(8,128)(2,1)S(1)}, bf16[528,256]{1,0:T(8,128)(2,1)S(1)}, u32[]{:S(2)}, u32[]{:S(2)}) collective-permute-start(bf16[528,256]{1,0:T(8,128)(2,1)S(1)} %shard_map.47.own_ref), channel_id=1, source_target_pairs={{256,0},{257,1},{258,2},{259,3},{260,4},{261,5},{262,6},{263,7},{2... | collective-permute-start | bytes 811016 | tf_op jit(solution)/shard_map/ppermute | solution.py:253
  25.8 2.3 %collective-permute-start.3 = (bf16[528,256]{1,0:T(8,128)(2,1)S(1)}, bf16[528,256]{1,0:T(8,128)(2,1)S(1)}, u32[]{:S(2)}, u32[]{:S(2)}) collective-permute-start(bf16[528,256]{1,0:T(8,128)(2,1)S(1)} %shard_map.47.own_ref), channel_id=1, source_target_pairs={{318,0},{319,1},{0,2},{1,3},{2,4},{3,5},{4,6},{5,7},{262,8},{263,9... | collective-permute-start | bytes 811016 | tf_op jit(solution)/shard_map/ppermute | solution.py:254
  28.1 2.7 %collective-permute-start.2 = (bf16[528,256]{1,0:T(8,128)(2,1)S(1)}, bf16[528,256]{1,0:T(8,128)(2,1)S(1)}, u32[]{:S(2)}, u32[]{:S(2)}) collective-permute-start(bf16[528,256]{1,0:T(8,128)(2,1)S(1)} %shard_map.47.own_ref), channel_id=1, source_target_pairs={{62,0},{63,1},{256,2},{257,3},{258,4},{259,5},{260,6},{261,7},{6,8... | collective-permute-start | bytes 811016 | tf_op jit(solution)/shard_map/ppermute | solution.py:255
  30.9 11.3 %collective-permute-done.other_ref.p1_ref = bf16[528,256]{1,0:T(8,128)(2,1)S(1)} collective-permute-done((bf16[528,256]{1,0:T(8,128)(2,1)S(1)}, bf16[528,256]{1,0:T(8,128)(2,1)S(1)}, u32[]{:S(2)}, u32[]{:S(2)}) %collective-permute-start) | collective-permute-done | bytes 270368 | tf_op jit(solution)/shard_map/ppermute | solution.py:253
  42.2 1.9 %collective-permute-start.1 = (bf16[528,256]{1,0:T(8,128)(2,1)S(1)}, bf16[528,256]{1,0:T(8,128)(2,1)S(1)}, u32[]{:S(2)}, u32[]{:S(2)}) collective-permute-start(bf16[528,256]{1,0:T(8,128)(2,1)S(1)} %shard_map.48), channel_id=1, source_target_pairs={{316,0},{317,1},{318,2},{319,3},{0,4},{1,5},{2,6},{3,7},{260,8},{2... | collective-permute-start | bytes 811016 | tf_op jit(solution)/shard_map/ppermute | solution.py:256
  44.1 8.9 %collective-permute-done.3.p2_ref = bf16[528,256]{1,0:T(8,128)(2,1)S(1)} collective-permute-done((bf16[528,256]{1,0:T(8,128)(2,1)S(1)}, bf16[528,256]{1,0:T(8,128)(2,1)S(1)}, u32[]{:S(2)}, u32[]{:S(2)}) %collective-permute-start.3) | collective-permute-done | bytes 270368 | tf_op jit(solution)/shard_map/ppermute | solution.py:254
  53.0 0.0 all-to-all-done
  53.0 6.6 %shard_map.49 = (f32[2,8,256,128]{3,2,1,0:T(8,128)S(1)}, f32[2,8,256,256]{3,2,1,0:T(8,128)S(1)}) custom-call(bf16[512,1024]{1,0:T(8,128)(2,1)S(1)} %bitcast.18, bf16[528,256]{1,0:T(8,128)(2,1)S(1)} %shard_map.47.own_ref, bf16[528,256]{1,0:T(8,128)(2,1)S(1)} %collective-permute-done.other_ref.p1_ref, bf16[528,256]{1,0:T(8,128)(2,1)S(1)} %collective-permute-done.3.p2_ref), custom_call_target="tpu_custom_call" | custom-call | flops 4294967296 | bytes 8388608 | tf_op jit(solution)/shard_map/pallas_call | solution.py:213
  59.6 5.2 %collective-permute-done.2.p4_ref = bf16[528,256]{1,0:T(8,128)(2,1)S(1)} collective-permute-done((bf16[528,256]{1,0:T(8,128)(2,1)S(1)}, bf16[528,256]{1,0:T(8,128)(2,1)S(1)}, u32[]{:S(2)}, u32[]{:S(2)}) %collective-permute-start.2) | collective-permute-done | bytes 270368 | tf_op jit(solution)/shard_map/ppermute | solution.py:255
  64.8 0.0 collective-permute-done.1.p3_ref
  64.8 4.1 %shard_map.50 = bf16[512,1024]{1,0:T(8,128)(2,1)S(1)} custom-call(bf16[512,1024]{1,0:T(8,128)(2,1)S(1)} %bitcast.19, bf16[528,256]{1,0:T(8,128)(2,1)S(1)} %shard_map.47.own_ref, bf16[528,256]{1,0:T(8,128)(2,1)S(1)} %collective-permute-done.1.p3_ref, bf16[528,256]{1,0:T(8,128)(2,1)S(1)} %collective-permute-done.2.p4_ref, ...), custom_call_target="tpu_custom_call" | custom-call | flops 2147483648 | bytes 8388608 | tf_op jit(solution)/shard_map/pallas_call | solution.py:231
  69.0 23.8 %all_to_all.35 = bf16[8,64,1024]{2,1,0:T(8,128)(2,1)S(1)} all-to-all(bf16[8,64,1024]{2,1,0:T(8,128)(2,1)S(1)} %bitcast.20), channel_id=1, replica_groups=mesh['yh'=2,'x'=4,'z'=8,'yl'=4,'c'=2] {'c','x'}, dimensions={0} | all-to-all | bytes 2097152 | tf_op jit(solution)/shard_map/all_to_all | solution.py:262
  92.8 1.1 %copy.8 = bf16[8,8,8,1024]{3,1,2,0:T(8,128)(2,1)} copy(bf16[8,8,8,1024]{3,1,0,2:T(8,128)(2,1)S(1)} %bitcast.21) | data formatting | bytes 2097152
  (2 shorter events, 0.0 us)
Async XLA Ops:
  1.7 17.1 %all-to-all-start.1 = ((bf16[8,72,256]{2,1,0:T(8,128)(2,1)}), bf16[8,72,256]{2,1,0:T(8,128)(2,1)S(1)}, u32[]{:S(2)}, u32[]{:S(2)}) async-start(bf16[8,72,256]{2,1,0:T(8,128)(2,1)} %shard_map.46), calls=%async_computation.1 | async-start | bytes 589824 | tf_op jit(solution)/shard_map/all_to_all | solution.py:251
  18.9 34.2 %all-to-all-start = ((bf16[64,8,1024]{2,0,1:T(8,128)(2,1)}), bf16[64,8,1024]{2,0,1:T(8,128)(2,1)S(1)}, u32[]{:S(2)}, u32[]{:S(2)}) async-start(bf16[64,8,1024]{2,0,1:T(8,128)(2,1)} %bitcast.17), calls=%async_computation | async-start | bytes 2097152 | tf_op jit(solution)/shard_map/all_to_all | solution.py:257
  22.7 19.4 %collective-permute-start = (bf16[528,256]{1,0:T(8,128)(2,1)S(1)}, bf16[528,256]{1,0:T(8,128)(2,1)S(1)}, u32[]{:S(2)}, u32[]{:S(2)}) collective-permute-start(bf16[528,256]{1,0:T(8,128)(2,1)S(1)} %shard_map.47.own_ref), channel_id=1, source_target_pairs={{256,0},{257,1},{258,2},{259,3},{260,4},{261,5},{262,6},{263,7},{2... | collective-permute-start | bytes 811016 | tf_op jit(solution)/shard_map/ppermute | solution.py:253
  25.8 27.2 %collective-permute-start.3 = (bf16[528,256]{1,0:T(8,128)(2,1)S(1)}, bf16[528,256]{1,0:T(8,128)(2,1)S(1)}, u32[]{:S(2)}, u32[]{:S(2)}) collective-permute-start(bf16[528,256]{1,0:T(8,128)(2,1)S(1)} %shard_map.47.own_ref), channel_id=1, source_target_pairs={{318,0},{319,1},{0,2},{1,3},{2,4},{3,5},{4,6},{5,7},{262,8},{263,9... | collective-permute-start | bytes 811016 | tf_op jit(solution)/shard_map/ppermute | solution.py:254
  28.1 36.7 %collective-permute-start.2 = (bf16[528,256]{1,0:T(8,128)(2,1)S(1)}, bf16[528,256]{1,0:T(8,128)(2,1)S(1)}, u32[]{:S(2)}, u32[]{:S(2)}) collective-permute-start(bf16[528,256]{1,0:T(8,128)(2,1)S(1)} %shard_map.47.own_ref), channel_id=1, source_target_pairs={{62,0},{63,1},{256,2},{257,3},{258,4},{259,5},{260,6},{261,7},{6,8... | collective-permute-start | bytes 811016 | tf_op jit(solution)/shard_map/ppermute | solution.py:255
  42.2 22.7 %collective-permute-start.1 = (bf16[528,256]{1,0:T(8,128)(2,1)S(1)}, bf16[528,256]{1,0:T(8,128)(2,1)S(1)}, u32[]{:S(2)}, u32[]{:S(2)}) collective-permute-start(bf16[528,256]{1,0:T(8,128)(2,1)S(1)} %shard_map.48), channel_id=1, source_target_pairs={{316,0},{317,1},{318,2},{319,3},{0,4},{1,5},{2,6},{3,7},{260,8},{2... | collective-permute-start | bytes 811016 | tf_op jit(solution)/shard_map/ppermute | solution.py:256

commit v2 on v1

v2 whole, which is shorter than its diff:
```python
import math

import jax
import jax.numpy as jnp
from jax import lax
from jax.experimental import pallas as pl
from jax.experimental.pallas import tpu as pltpu
from jax.sharding import Mesh
from jax.sharding import PartitionSpec as P

HEAD_DIMENSION = 128
RUN = 256
ROWS = 64
FLAG_ROWS = 8
GROUP = 8
SCALE = math.log2(math.e) / math.sqrt(HEAD_DIMENSION)
NEG_BIG = -1e30
AXES = ("yh", "x", "z", "yl", "c")
SIZES = (2, 4, 8, 4, 2)
MIB = 1024 * 1024


def ring_route(shift, back):
    nyh, nx, nz, nyl, nc = SIZES
    route = []
    for yh in range(nyh):
        for x in range(nx):
            for z in range(nz):
                for yl in range(nyl):
                    for c in range(nc):
                        ring = (yh * nyl + yl - shift) % (nyh * nyl)
                        chain = (z * nyl + yl - back) % (nz * nyl)
                        z2, yl2 = divmod(chain, nyl)
                        src = (((ring // nyl * nx + x) * nz + z2) * nyl + yl2) * nc + c
                        dst = (((yh * nx + x) * nz + z) * nyl + yl) * nc + c
                        route.append((src, dst))
    return route


def vmem(count):
    return [pl.BlockSpec(memory_space=pltpu.VMEM)] * count


def smem():
    return [pl.BlockSpec(memory_space=pltpu.SMEM)]


def pack_kernel(pos_ref, k_ref, v_ref, out_ref):
    run = jnp.right_shift(pos_ref[0], 8).astype(jnp.float32)
    flags = jnp.full((FLAG_ROWS, 256), run, jnp.float32).astype(jnp.bfloat16)
    for g in range(8):
        lanes = slice(g * 128, (g + 1) * 128)
        both = jnp.concatenate([k_ref[:, lanes], v_ref[:, lanes]], axis=1)
        out_ref[g] = jnp.concatenate([both, flags], axis=0)


def pack(positions, key_tensor, value_tensor):
    return pl.pallas_call(
        pack_kernel,
        out_shape=jax.ShapeDtypeStruct((8, ROWS + FLAG_ROWS, 256), jnp.bfloat16),
        in_specs=smem() + vmem(2),
        out_specs=vmem(1)[0],
        compiler_params=pltpu.CompilerParams(vmem_limit_bytes=56 * MIB),
    )(positions, key_tensor, value_tensor)


def repack_kernel(in_ref, out_ref):
    flags = []
    for c in range(2):
        for x in range(4):
            block = in_ref[c * 4 + x]
            at = c * RUN + x * ROWS
            out_ref[at : at + ROWS, :] = block[0:ROWS, :]
        flags.append(block[ROWS : ROWS + FLAG_ROWS, 0:128])
    line = jnp.concatenate(flags, axis=1)
    out_ref[2 * RUN : 2 * RUN + 16, :] = jnp.concatenate([line, line], axis=0)


def relay_kernel(own_ref, other_ref, out_ref):
    last = slice(2 * RUN, 2 * RUN + 16)
    out_ref[0:RUN, :] = own_ref[RUN : 2 * RUN, :]
    out_ref[RUN : 2 * RUN, :] = other_ref[RUN : 2 * RUN, :]
    out_ref[last, 0:128] = own_ref[last, 128:256]
    out_ref[last, 128:256] = other_ref[last, 128:256]


def rearrange(kernel, *operands):
    return pl.pallas_call(
        kernel,
        out_shape=jax.ShapeDtypeStruct((2 * RUN + 16, 256), jnp.bfloat16),
        in_specs=vmem(len(operands)),
        out_specs=vmem(1)[0],
        compiler_params=pltpu.CompilerParams(vmem_limit_bytes=4 * MIB),
    )(*operands)


def flag(ref, half):
    rows = ref.shape[0]
    tile = ref[rows - 16 : rows, half * 128 : (half + 1) * 128].astype(jnp.float32)
    return jnp.max(tile).astype(jnp.int32)


def gather_visible(slots, own_run, kv_ref, i, start):
    count = jnp.int32(start)
    for ref, row, run in slots:
        seen = run < own_run
        at = count

        @pl.when(seen)
        def _(ref=ref, row=row, at=at):
            kv_ref[i, at] = ref[row : row + RUN, :]

        count = count + seen.astype(jnp.int32)
    return count


def lane_fold(s):
    return jnp.maximum(s[:, 0:128], s[:, 128:256])


def scores(q, keys):
    return lax.dot_general(q, keys, (((1,), (1,)), ((), ())), preferred_element_type=jnp.float32)


def queries_of(q_ref, i, h):
    return q_ref[pl.ds(pl.multiple_of(i * RUN, RUN), RUN), h * 128 : (h + 1) * 128]


def head_rows(h):
    return slice(h * RUN, (h + 1) * RUN)


def weighted(s_ref, m_ref, kv_ref, i, at, rows):
    m = m_ref[i, rows, :]
    weights, values = [], []
    for j in at:
        for lanes in (slice(0, 128), slice(128, 256)):
            weights.append(jnp.exp2((s_ref[j, rows, lanes] - m) * SCALE).astype(jnp.bfloat16))
        values.append(kv_ref[i, j, :, 128:256])
    values = jnp.concatenate(values, axis=0)
    values = jnp.concatenate([values, jnp.ones(values.shape, jnp.bfloat16)], axis=1)
    return jnp.dot(jnp.concatenate(weights, axis=1), values, preferred_element_type=jnp.float32)


def row_max(m):
    return jnp.broadcast_to(jnp.max(m, axis=1, keepdims=True), m.shape)


def first_kernel(q_ref, own_ref, other_ref, p2_ref, m_ref, acc_ref, kv_ref, s_ref):
    runs = [flag(own_ref, c) for c in range(2)]
    other = [(other_ref, c * RUN, 127 - runs[c]) for c in range(2)]
    near = [(p2_ref, c * RUN, flag(p2_ref, c)) for c in range(2)]
    slots = [[other[0]] + near, [other[1], (own_ref, 0, runs[0]), other[0]] + near]
    counts = []
    for i in range(2):
        kv_ref[i, 0] = own_ref[i * RUN : (i + 1) * RUN, :]
        counts.append(gather_visible(slots[i], runs[i], kv_ref, i, 1))
    lower = lax.broadcasted_iota(jnp.int32, (RUN, RUN), 0) >= lax.broadcasted_iota(
        jnp.int32, (RUN, RUN), 1
    )

    @pl.loop(0, 2)
    def _(i):
        count = jnp.where(i == 0, counts[0], counts[1])
        for h in range(GROUP):
            s = jnp.where(lower, scores(queries_of(q_ref, i, h), kv_ref[i, 0, :, 0:128]), NEG_BIG)
            s_ref[0, head_rows(h), :] = s
            m_ref[i, head_rows(h), :] = lane_fold(s)

        @pl.loop(1, count)
        def _(j):
            for h in range(GROUP):
                s = scores(queries_of(q_ref, i, h), kv_ref[i, j, :, 0:128])
                s_ref[j, head_rows(h), :] = s
                m_ref[i, head_rows(h), :] = jnp.maximum(m_ref[i, head_rows(h), :], lane_fold(s))

        for h in range(GROUP):
            m_ref[i, head_rows(h), :] = row_max(m_ref[i, head_rows(h), :])
            acc_ref[i, head_rows(h), :] = weighted(s_ref, m_ref, kv_ref, i, [0], head_rows(h))

        @pl.loop(1, count)
        def _(j):
            for h in range(GROUP):
                acc_ref[i, head_rows(h), :] = acc_ref[i, head_rows(h), :] + weighted(
                    s_ref, m_ref, kv_ref, i, [j], head_rows(h)
                )


def second_kernel(
    q_ref, own_ref, p4_ref, p3_ref, m1_ref, acc1_ref, out_ref, m_ref, acc_ref, kv_ref, s_ref
):
    runs = [flag(own_ref, c) for c in range(2)]
    near = [(p4_ref, c * RUN, flag(p4_ref, c)) for c in range(2)]
    far = [(p3_ref, c * RUN, flag(p3_ref, c)) for c in range(2)]
    slots = [near + far, near]
    counts = [gather_visible(slots[i], runs[i], kv_ref, i, 0) for i in range(2)]

    @pl.loop(0, 2)
    def _(i):
        count = jnp.where(i == 0, counts[0], counts[1])
        for h in range(GROUP):
            m_ref[i, head_rows(h), :] = m1_ref[i, head_rows(h), :]

        @pl.loop(0, count)
        def _(j):
            for h in range(GROUP):
                s = scores(queries_of(q_ref, i, h), kv_ref[i, j, :, 0:128])
                s_ref[j, head_rows(h), :] = s
                m_ref[i, head_rows(h), :] = jnp.maximum(m_ref[i, head_rows(h), :], lane_fold(s))

        for h in range(GROUP):
            m = row_max(m_ref[i, head_rows(h), :])
            m_ref[i, head_rows(h), :] = m
            rescale = jnp.exp2((m1_ref[i, head_rows(h), :] - m) * SCALE)
            for lanes in (slice(0, 128), slice(128, 256)):
                acc_ref[head_rows(h), lanes] = acc1_ref[i, head_rows(h), lanes] * rescale
        odd = count % 2

        @pl.when(odd == 1)
        def _():
            for h in range(GROUP):
                acc_ref[head_rows(h), :] = acc_ref[head_rows(h), :] + weighted(
                    s_ref, m_ref, kv_ref, i, [0], head_rows(h)
                )

        @pl.loop(0, count // 2)
        def _(pair):
            j = odd + 2 * pair
            for h in range(GROUP):
                acc_ref[head_rows(h), :] = acc_ref[head_rows(h), :] + weighted(
                    s_ref, m_ref, kv_ref, i, [j, j + 1], head_rows(h)
                )

        at = pl.ds(pl.multiple_of(i * RUN, RUN), RUN)
        for h in range(GROUP):
            block = acc_ref[head_rows(h), :]
            out_ref[at, h * 128 : (h + 1) * 128] = (block[:, 0:128] / block[:, 128:256]).astype(
                jnp.bfloat16
            )


def first_part(*operands):
    return pl.pallas_call(
        first_kernel,
        out_shape=(
            jax.ShapeDtypeStruct((2, GROUP * RUN, 128), jnp.float32),
            jax.ShapeDtypeStruct((2, GROUP * RUN, 256), jnp.float32),
        ),
        in_specs=vmem(4),
        out_specs=tuple(vmem(2)),
        scratch_shapes=[
            pltpu.VMEM((2, 6, RUN, 256), jnp.bfloat16),
            pltpu.VMEM((6, GROUP * RUN, 256), jnp.float32),
        ],
        compiler_params=pltpu.CompilerParams(vmem_limit_bytes=20 * MIB),
        cost_estimate=pl.CostEstimate(flops=4 << 29, bytes_accessed=8 << 20, transcendentals=2 << 20),
    )(*operands)


def second_part(*operands):
    return pl.pallas_call(
        second_kernel,
        out_shape=jax.ShapeDtypeStruct((2 * RUN, GROUP * 128), jnp.bfloat16),
        in_specs=vmem(6),
        out_specs=vmem(1)[0],
        scratch_shapes=[
            pltpu.VMEM((2, GROUP * RUN, 128), jnp.float32),
            pltpu.VMEM((GROUP * RUN, 256), jnp.float32),
            pltpu.VMEM((2, 4, RUN, 256), jnp.bfloat16),
            pltpu.VMEM((4, GROUP * RUN, 256), jnp.float32),
        ],
        compiler_params=pltpu.CompilerParams(vmem_limit_bytes=22 * MIB),
        cost_estimate=pl.CostEstimate(flops=4 << 29, bytes_accessed=8 << 20, transcendentals=2 << 20),
    )(*operands)


def body(queries, key_tensor, value_tensor, positions):
    group = ("c", "x")
    packed = pack(positions, key_tensor, value_tensor)
    own = rearrange(
        repack_kernel, lax.all_to_all(packed, group, split_axis=0, concat_axis=0, tiled=True)
    )
    p1 = lax.ppermute(own, AXES, ring_route(4, 0))
    p4 = lax.ppermute(own, AXES, ring_route(5, 1))
    p2 = lax.ppermute(own, AXES, ring_route(1, 1))
    p3 = lax.ppermute(rearrange(relay_kernel, own, p1), AXES, ring_route(2, 2))
    q = lax.all_to_all(
        queries.reshape(ROWS, 8, GROUP * 128), group, split_axis=1, concat_axis=0, tiled=True
    ).reshape(2 * RUN, GROUP * 128)
    m1, acc1 = first_part(q, own, p1, p2)
    out = second_part(q, own, p4, p3, m1, acc1)
    result = lax.all_to_all(
        out.reshape(8, ROWS, GROUP * 128), group, split_axis=0, concat_axis=2, tiled=True
    )
    return result.reshape(ROWS, 8 * GROUP * 128)


def solution(mesh):
    finer = Mesh(mesh.devices.reshape(SIZES), AXES)
    return jax.shard_map(
        body,
        mesh=finer,
        in_specs=(P(AXES, None), P(AXES, None), P(AXES, None), P(AXES)),
        out_specs=P(AXES, None),
        check_vma=False,
    )
```

time: 94.3 us -> 91.1 us (0.966)
  blocking collectives: 23.8 us -> 19.4 us
  waiting for transfers between devices: 30.1 us -> 34.5 us
  Pallas kernels: 12.5 us -> 8.78 us
    ppermute x1, waiting for transfers between devices: 5.21 us -> 9.65 us  [body(): p4 = lax.ppermute(own, AXES, ring_route(5, 1))]
    pallas_call x1, Pallas kernels: 6.6 us -> 2.15 us  [first_part(): pl.pallas_call(first_kernel, out_shape=(jax.ShapeDtypeStruct((2, GROUP *...]
    all_to_all x1, blocking collectives: 23.8 us -> 19.4 us  [body(): lax.all_to_all(out.reshape(8, ROWS, GROUP * 128), group, split_axis=0, co...]
  transfers between devices with their start and end apart: 6 -> 6, of which waited for: 4 -> 4; matrix products, arithmetic and copies ran while one was open for 2% -> 3% of each run, Pallas kernels for 7% -> 2%
where the time goes in v2:
time: 91.1 us; the launch traced here: 90.2 us
  waiting for transfers between devices  34.5 us (38%)
  starting transfers between devices  24.1 us (26%)
  blocking collectives  19.4 us (21%)
  Pallas kernels  8.78 us (10%)
  local copies, waits for them, and re-layouts  3.35 us (4%)
    all_to_all x1, blocking collectives, body(): lax.all_to_all(out.reshape(8, ROWS, GROUP * 128), group, split_axis=0, co...  19.4 us
    ppermute x1, waiting for transfers between devices, body(): p1 = lax.ppermute(own, AXES, ring_route(4, 0))  11.3 us
    all_to_all x1, starting transfers between devices, body(): lax.all_to_all(packed, group, split_axis=0, concat_axis=0, tiled=True)  10.2 us
    ppermute x1, waiting for transfers between devices, body(): p4 = lax.ppermute(own, AXES, ring_route(5, 1))  9.65 us
    ppermute x1, waiting for transfers between devices, body(): p2 = lax.ppermute(own, AXES, ring_route(1, 1))  8.94 us
    pallas_call x1, Pallas kernels, second_part(): pl.pallas_call(second_kernel, out_shape=jax.ShapeDtypeStruct((2 * RUN, GR...  4.86 us
    all_to_all x1, waiting for transfers between devices, body(): lax.all_to_all(packed, group, split_axis=0, concat_axis=0, tiled=True)  4.63 us
    all_to_all x1, starting transfers between devices, body(): lax.all_to_all(queries.reshape(ROWS, 8, GROUP * 128), group, split_axis=1...  3.85 us
  transfers between devices with their start and end apart: 6, of which 4 were waited for; matrix products, arithmetic and copies ran while one was open for 3% of the time, Pallas kernels for 2%

profile of v2, /device:TPU:1, one launch (start us, length us, event | category | flops | bytes accessed | tf_op | source)
XLA Modules:
  0.0 90.2 jit_solution(5516647870432628546)
XLA Ops:
  0.0 1.7 %shard_map.46 = bf16[8,72,256]{2,1,0:T(8,128)(2,1)} custom-call(s32[64]{0:T(128)} %pos_ref.1, bf16[64,1024]{1,0:T(8,128)(2,1)} %k_ref.1, bf16[64,1024]{1,0:T(8,128)(2,1)} %v_ref.1), custom_call_target="tpu_custom_call" | custom-call | tf_op jit(solution)/shard_map/pallas_call | solution.py:58
  1.7 10.2 %all-to-all-start.1 = ((bf16[8,72,256]{2,1,0:T(8,128)(2,1)}), bf16[8,72,256]{2,1,0:T(8,128)(2,1)S(1)}, u32[]{:S(2)}, u32[]{:S(2)}) async-start(bf16[8,72,256]{2,1,0:T(8,128)(2,1)} %shard_map.46), calls=%async_computation.1 | async-start | bytes 589824 | tf_op jit(solution)/shard_map/all_to_all | solution.py:281
  12.0 2.3 %copy.11 = bf16[8,8,8,1024]{3,2,0,1:T(8,128)(2,1)} copy(bf16[8,8,8,1024]{3,2,1,0:T(8,128)(2,1)} %bitcast.22) | data formatting | bytes 2097152 | tf_op jit(solution)/shard_map/reshape | solution.py:288
  14.2 4.6 %all-to-all-done.1.in_ref = bf16[8,72,256]{2,1,0:T(8,128)(2,1)S(1)} async-done(((bf16[8,72,256]{2,1,0:T(8,128)(2,1)}), bf16[8,72,256]{2,1,0:T(8,128)(2,1)S(1)}, u32[]{:S(2)}, u32[]{:S(2)}) %all-to-all-start.1) | async-done | bytes 294944 | tf_op jit(solution)/shard_map/all_to_all | solution.py:281
  18.9 3.8 %all-to-all-start = ((bf16[64,8,1024]{2,0,1:T(8,128)(2,1)}), bf16[64,8,1024]{2,0,1:T(8,128)(2,1)S(1)}, u32[]{:S(2)}, u32[]{:S(2)}) async-start(bf16[64,8,1024]{2,0,1:T(8,128)(2,1)} %bitcast.17), calls=%async_computation | async-start | bytes 2097152 | tf_op jit(solution)/shard_map/all_to_all | solution.py:287
  22.7 3.0 %collective-permute-start.1 = (bf16[528,256]{1,0:T(8,128)(2,1)S(1)}, bf16[528,256]{1,0:T(8,128)(2,1)S(1)}, u32[]{:S(2)}, u32[]{:S(2)}) collective-permute-start(bf16[528,256]{1,0:T(8,128)(2,1)S(1)} %shard_map.47.own_ref), channel_id=1, source_target_pairs={{256,0},{257,1},{258,2},{259,3},{260,4},{261,5},{262,6},{263,7},{2... | collective-permute-start | bytes 811016 | tf_op jit(solution)/shard_map/ppermute | solution.py:283
  25.8 2.3 %collective-permute-start.3 = (bf16[528,256]{1,0:T(8,128)(2,1)S(1)}, bf16[528,256]{1,0:T(8,128)(2,1)S(1)}, u32[]{:S(2)}, u32[]{:S(2)}) collective-permute-start(bf16[528,256]{1,0:T(8,128)(2,1)S(1)} %shard_map.47.own_ref), channel_id=1, source_target_pairs={{318,0},{319,1},{0,2},{1,3},{2,4},{3,5},{4,6},{5,7},{262,8},{263,9... | collective-permute-start | bytes 811016 | tf_op jit(solution)/shard_map/ppermute | solution.py:285
  28.1 2.7 %collective-permute-start = (bf16[528,256]{1,0:T(8,128)(2,1)S(1)}, bf16[528,256]{1,0:T(8,128)(2,1)S(1)}, u32[]{:S(2)}, u32[]{:S(2)}) collective-permute-start(bf16[528,256]{1,0:T(8,128)(2,1)S(1)} %shard_map.47.own_ref), channel_id=1, source_target_pairs={{62,0},{63,1},{256,2},{257,3},{258,4},{259,5},{260,6},{261,7},{6,8... | collective-permute-start | bytes 811016 | tf_op jit(solution)/shard_map/ppermute | solution.py:284
  30.9 11.3 %collective-permute-done.1.other_ref = bf16[528,256]{1,0:T(8,128)(2,1)S(1)} collective-permute-done((bf16[528,256]{1,0:T(8,128)(2,1)S(1)}, bf16[528,256]{1,0:T(8,128)(2,1)S(1)}, u32[]{:S(2)}, u32[]{:S(2)}) %collective-permute-start.1) | collective-permute-done | bytes 270368 | tf_op jit(solution)/shard_map/ppermute | solution.py:283
  42.2 1.9 %collective-permute-start.2 = (bf16[528,256]{1,0:T(8,128)(2,1)S(1)}, bf16[528,256]{1,0:T(8,128)(2,1)S(1)}, u32[]{:S(2)}, u32[]{:S(2)}) collective-permute-start(bf16[528,256]{1,0:T(8,128)(2,1)S(1)} %shard_map.48), channel_id=1, source_target_pairs={{316,0},{317,1},{318,2},{319,3},{0,4},{1,5},{2,6},{3,7},{260,8},{2... | collective-permute-start | bytes 811016 | tf_op jit(solution)/shard_map/ppermute | solution.py:286
  44.1 8.9 %collective-permute-done.3.p2_ref = bf16[528,256]{1,0:T(8,128)(2,1)S(1)} collective-permute-done((bf16[528,256]{1,0:T(8,128)(2,1)S(1)}, bf16[528,256]{1,0:T(8,128)(2,1)S(1)}, u32[]{:S(2)}, u32[]{:S(2)}) %collective-permute-start.3) | collective-permute-done | bytes 270368 | tf_op jit(solution)/shard_map/ppermute | solution.py:285
  53.0 0.0 all-to-all-done
  53.0 2.2 %shard_map.49 = (f32[2,2048,128]{2,1,0:T(8,128)S(1)}, f32[2,2048,256]{2,1,0:T(8,128)S(1)}) custom-call(bf16[512,1024]{1,0:T(8,128)(2,1)S(1)} %bitcast.18, bf16[528,256]{1,0:T(8,128)(2,1)S(1)} %shard_map.47.own_ref, bf16[528,256]{1,0:T(8,128)(2,1)S(1)} %collective-permute-done.1.other_ref, bf16[528,256]{1,0:T(8,128)(2,1)S(1)} %collective-permute-done.3.p2_ref), custom_call_target="tpu_custom_call" | custom-call | flops 2147483648 | bytes 8388608 | tf_op jit(solution)/shard_map/pallas_call | solution.py:243
  55.2 9.7 %collective-permute-done.p4_ref = bf16[528,256]{1,0:T(8,128)(2,1)S(1)} collective-permute-done((bf16[528,256]{1,0:T(8,128)(2,1)S(1)}, bf16[528,256]{1,0:T(8,128)(2,1)S(1)}, u32[]{:S(2)}, u32[]{:S(2)}) %collective-permute-start) | collective-permute-done | bytes 270368 | tf_op jit(solution)/shard_map/ppermute | solution.py:284
  64.8 0.0 collective-permute-done.2.p3_ref
  64.8 4.9 %shard_map.50 = bf16[512,1024]{1,0:T(8,128)(2,1)S(1)} custom-call(bf16[512,1024]{1,0:T(8,128)(2,1)S(1)} %bitcast.19, bf16[528,256]{1,0:T(8,128)(2,1)S(1)} %shard_map.47.own_ref, bf16[528,256]{1,0:T(8,128)(2,1)S(1)} %collective-permute-done.p4_ref, bf16[528,256]{1,0:T(8,128)(2,1)S(1)} %collective-permute-done.2.p3_ref, ...), custom_call_target="tpu_custom_call" | custom-call | flops 2147483648 | bytes 8388608 | tf_op jit(solution)/shard_map/pallas_call | solution.py:261
  69.7 19.4 %all_to_all.35 = bf16[8,64,1024]{2,1,0:T(8,128)(2,1)S(1)} all-to-all(bf16[8,64,1024]{2,1,0:T(8,128)(2,1)S(1)} %bitcast.20), channel_id=1, replica_groups=mesh['yh'=2,'x'=4,'z'=8,'yl'=4,'c'=2] {'c','x'}, dimensions={0} | all-to-all | bytes 2097152 | tf_op jit(solution)/shard_map/all_to_all | solution.py:292
  89.1 1.1 %copy.8 = bf16[8,8,8,1024]{3,1,2,0:T(8,128)(2,1)} copy(bf16[8,8,8,1024]{3,1,0,2:T(8,128)(2,1)S(1)} %bitcast.21) | data formatting | bytes 2097152
  (2 shorter events, 0.0 us)
Async XLA Ops:
  1.7 17.1 %all-to-all-start.1 = ((bf16[8,72,256]{2,1,0:T(8,128)(2,1)}), bf16[8,72,256]{2,1,0:T(8,128)(2,1)S(1)}, u32[]{:S(2)}, u32[]{:S(2)}) async-start(bf16[8,72,256]{2,1,0:T(8,128)(2,1)} %shard_map.46), calls=%async_computation.1 | async-start | bytes 589824 | tf_op jit(solution)/shard_map/all_to_all | solution.py:281
  18.9 34.2 %all-to-all-start = ((bf16[64,8,1024]{2,0,1:T(8,128)(2,1)}), bf16[64,8,1024]{2,0,1:T(8,128)(2,1)S(1)}, u32[]{:S(2)}, u32[]{:S(2)}) async-start(bf16[64,8,1024]{2,0,1:T(8,128)(2,1)} %bitcast.17), calls=%async_computation | async-start | bytes 2097152 | tf_op jit(solution)/shard_map/all_to_all | solution.py:287
  22.7 19.4 %collective-permute-start.1 = (bf16[528,256]{1,0:T(8,128)(2,1)S(1)}, bf16[528,256]{1,0:T(8,128)(2,1)S(1)}, u32[]{:S(2)}, u32[]{:S(2)}) collective-permute-start(bf16[528,256]{1,0:T(8,128)(2,1)S(1)} %shard_map.47.own_ref), channel_id=1, source_target_pairs={{256,0},{257,1},{258,2},{259,3},{260,4},{261,5},{262,6},{263,7},{2... | collective-permute-start | bytes 811016 | tf_op jit(solution)/shard_map/ppermute | solution.py:283
  25.8 27.2 %collective-permute-start.3 = (bf16[528,256]{1,0:T(8,128)(2,1)S(1)}, bf16[528,256]{1,0:T(8,128)(2,1)S(1)}, u32[]{:S(2)}, u32[]{:S(2)}) collective-permute-start(bf16[528,256]{1,0:T(8,128)(2,1)S(1)} %shard_map.47.own_ref), channel_id=1, source_target_pairs={{318,0},{319,1},{0,2},{1,3},{2,4},{3,5},{4,6},{5,7},{262,8},{263,9... | collective-permute-start | bytes 811016 | tf_op jit(solution)/shard_map/ppermute | solution.py:285
  28.1 36.7 %collective-permute-start = (bf16[528,256]{1,0:T(8,128)(2,1)S(1)}, bf16[528,256]{1,0:T(8,128)(2,1)S(1)}, u32[]{:S(2)}, u32[]{:S(2)}) collective-permute-start(bf16[528,256]{1,0:T(8,128)(2,1)S(1)} %shard_map.47.own_ref), channel_id=1, source_target_pairs={{62,0},{63,1},{256,2},{257,3},{258,4},{259,5},{260,6},{261,7},{6,8... | collective-permute-start | bytes 811016 | tf_op jit(solution)/shard_map/ppermute | solution.py:284
  42.2 22.7 %collective-permute-start.2 = (bf16[528,256]{1,0:T(8,128)(2,1)S(1)}, bf16[528,256]{1,0:T(8,128)(2,1)S(1)}, u32[]{:S(2)}, u32[]{:S(2)}) collective-permute-start(bf16[528,256]{1,0:T(8,128)(2,1)S(1)} %shard_map.48), channel_id=1, source_target_pairs={{316,0},{317,1},{318,2},{319,3},{0,4},{1,5},{2,6},{3,7},{260,8},{2... | collective-permute-start | bytes 811016 | tf_op jit(solution)/shard_map/ppermute | solution.py:286

commit v3 on v2

--- a/solution.py
+++ b/solution.py
@@ -1,3 +1,4 @@
+import functools
 import math
 
 import jax
@@ -68,7 +69,7 @@
     flags = []
     for c in range(2):
         for x in range(4):
-            block = in_ref[c * 4 + x]
+            block = in_ref[x * 2 + c]
             at = c * RUN + x * ROWS
             out_ref[at : at + ROWS, :] = block[0:ROWS, :]
         flags.append(block[ROWS : ROWS + FLAG_ROWS, 0:128])
@@ -123,7 +124,7 @@
 
 
 def queries_of(q_ref, i, h):
-    return q_ref[pl.ds(pl.multiple_of(i * RUN, RUN), RUN), h * 128 : (h + 1) * 128]
+    return q_ref[:, i, :, h * 128 : (h + 1) * 128].reshape(RUN, 128)
 
 
 def head_rows(h):
@@ -187,56 +188,73 @@
 
 
 def second_kernel(
-    q_ref, own_ref, p4_ref, p3_ref, m1_ref, acc1_ref, out_ref, m_ref, acc_ref, kv_ref, s_ref
+    mine, core_ref, q_ref, own_ref, p4_ref, p3_ref, m1_ref, acc1_ref, out_ref, m_ref, acc_ref, kv_ref, s_ref
 ):
-    runs = [flag(own_ref, c) for c in range(2)]
+    i = core_ref[0] if mine else 1 - core_ref[0]
+    own_run = jnp.where(i == 0, flag(own_ref, 0), flag(own_ref, 1))
     near = [(p4_ref, c * RUN, flag(p4_ref, c)) for c in range(2)]
-    far = [(p3_ref, c * RUN, flag(p3_ref, c)) for c in range(2)]
-    slots = [near + far, near]
-    counts = [gather_visible(slots[i], runs[i], kv_ref, i, 0) for i in range(2)]
-
-    @pl.loop(0, 2)
-    def _(i):
-        count = jnp.where(i == 0, counts[0], counts[1])
-        for h in range(GROUP):
-            m_ref[i, head_rows(h), :] = m1_ref[i, head_rows(h), :]
-
-        @pl.loop(0, count)
-        def _(j):
-            for h in range(GROUP):
-                s = scores(queries_of(q_ref, i, h), kv_ref[i, j, :, 0:128])
-                s_ref[j, head_rows(h), :] = s
-                m_ref[i, head_rows(h), :] = jnp.maximum(m_ref[i, head_rows(h), :], lane_fold(s))
-
-        for h in range(GROUP):
-            m = row_max(m_ref[i, head_rows(h), :])
-            m_ref[i, head_rows(h), :] = m
-            rescale = jnp.exp2((m1_ref[i, head_rows(h), :] - m) * SCALE)
-            for lanes in (slice(0, 128), slice(128, 256)):
-                acc_ref[head_rows(h), lanes] = acc1_ref[i, head_rows(h), lanes] * rescale
-        odd = count % 2
-
-        @pl.when(odd == 1)
-        def _():
-            for h in range(GROUP):
-                acc_ref[head_rows(h), :] = acc_ref[head_rows(h), :] + weighted(
-                    s_ref, m_ref, kv_ref, i, [0], head_rows(h)
-                )
-
-        @pl.loop(0, count // 2)
-        def _(pair):
-            j = odd + 2 * pair
-            for h in range(GROUP):
-                acc_ref[head_rows(h), :] = acc_ref[head_rows(h), :] + weighted(
-                    s_ref, m_ref, kv_ref, i, [j, j + 1], head_rows(h)
-                )
-
-        at = pl.ds(pl.multiple_of(i * RUN, RUN), RUN)
-        for h in range(GROUP):
-            block = acc_ref[head_rows(h), :]
-            out_ref[at, h * 128 : (h + 1) * 128] = (block[:, 0:128] / block[:, 128:256]).astype(
-                jnp.bfloat16
+    far = [(p3_ref, c * RUN, jnp.where(i == 0, flag(p3_ref, c), 128)) for c in range(2)]
+    count = gather_visible(near + far, own_run, kv_ref, 0, 0)
+    for h in range(GROUP):
+        m_ref[0, head_rows(h), :] = m1_ref[i, head_rows(h), :]
+
+    @pl.loop(0, count)
+    def _(j):
+        for h in range(GROUP):
+            s = scores(queries_of(q_ref, i, h), kv_ref[0, j, :, 0:128])
+            s_ref[j, head_rows(h), :] = s
+            m_ref[0, head_rows(h), :] = jnp.maximum(m_ref[0, head_rows(h), :], lane_fold(s))
+
+    for h in range(GROUP):
+        m = row_max(m_ref[0, head_rows(h), :])
+        m_ref[0, head_rows(h), :] = m
+        rescale = jnp.exp2((m1_ref[i, head_rows(h), :] - m) * SCALE)
+        for lanes in (slice(0, 128), slice(128, 256)):
+            acc_ref[head_rows(h), lanes] = acc1_ref[i, head_rows(h), lanes] * rescale
+    odd = count % 2
+
+    @pl.when(odd == 1)
+    def _():
+        for h in range(GROUP):
+            acc_ref[head_rows(h), :] = acc_ref[head_rows(h), :] + weighted(
+                s_ref, m_ref, kv_ref, 0, [0], head_rows(h)
             )
+
+    @pl.loop(0, count // 2)
+    def _(pair):
+        j = odd + 2 * pair
+        for h in range(GROUP):
+            acc_ref[head_rows(h), :] = acc_ref[head_rows(h), :] + weighted(
+                s_ref, m_ref, kv_ref, 0, [j, j + 1], head_rows(h)
+            )
+
+    for h in range(GROUP):
+        block = acc_ref[head_rows(h), :]
+        out_ref[:, h * 128 : (h + 1) * 128] = (block[:, 0:128] / block[:, 128:256]).astype(
+            jnp.bfloat16
+        )
+
+
+def join_kernel(core_ref, mine_ref, theirs_ref, out_ref):
+    @pl.when(core_ref[0] == 0)
+    def _():
+        out_ref[:, 0 : GROUP * 128] = mine_ref[...]
+        out_ref[:, GROUP * 128 : 2 * GROUP * 128] = theirs_ref[...]
+
+    @pl.when(core_ref[0] == 1)
+    def _():
+        out_ref[:, 0 : GROUP * 128] = theirs_ref[...]
+        out_ref[:, GROUP * 128 : 2 * GROUP * 128] = mine_ref[...]
+
+
+def join(core, mine, theirs):
+    return pl.pallas_call(
+        join_kernel,
+        out_shape=jax.ShapeDtypeStruct((RUN, 2 * GROUP * 128), jnp.bfloat16),
+        in_specs=smem() + vmem(2),
+        out_specs=vmem(1)[0],
+        compiler_params=pltpu.CompilerParams(vmem_limit_bytes=4 * MIB),
+    )(core, mine, theirs)
 
 
 def first_part(*operands):
@@ -257,25 +275,25 @@
     )(*operands)
 
 
-def second_part(*operands):
-    return pl.pallas_call(
-        second_kernel,
-        out_shape=jax.ShapeDtypeStruct((2 * RUN, GROUP * 128), jnp.bfloat16),
-        in_specs=vmem(6),
+def second_part(mine, *operands):
+    return pl.pallas_call(
+        functools.partial(second_kernel, mine),
+        out_shape=jax.ShapeDtypeStruct((RUN, GROUP * 128), jnp.bfloat16),
+        in_specs=smem() + vmem(6),
         out_specs=vmem(1)[0],
         scratch_shapes=[
-            pltpu.VMEM((2, GROUP * RUN, 128), jnp.float32),
+            pltpu.VMEM((1, GROUP * RUN, 128), jnp.float32),
             pltpu.VMEM((GROUP * RUN, 256), jnp.float32),
-            pltpu.VMEM((2, 4, RUN, 256), jnp.bfloat16),
+            pltpu.VMEM((1, 4, RUN, 256), jnp.bfloat16),
             pltpu.VMEM((4, GROUP * RUN, 256), jnp.float32),
         ],
-        compiler_params=pltpu.CompilerParams(vmem_limit_bytes=22 * MIB),
-        cost_estimate=pl.CostEstimate(flops=4 << 29, bytes_accessed=8 << 20, transcendentals=2 << 20),
+        compiler_params=pltpu.CompilerParams(vmem_limit_bytes=16 * MIB),
+        cost_estimate=pl.CostEstimate(flops=2 << 29, bytes_accessed=8 << 20, transcendentals=1 << 20),
     )(*operands)
 
 
 def body(queries, key_tensor, value_tensor, positions):
-    group = ("c", "x")
+    group = ("x", "c")
     packed = pack(positions, key_tensor, value_tensor)
     own = rearrange(
         repack_kernel, lax.all_to_all(packed, group, split_axis=0, concat_axis=0, tiled=True)
@@ -286,13 +304,14 @@
     p3 = lax.ppermute(rearrange(relay_kernel, own, p1), AXES, ring_route(2, 2))
     q = lax.all_to_all(
         queries.reshape(ROWS, 8, GROUP * 128), group, split_axis=1, concat_axis=0, tiled=True
-    ).reshape(2 * RUN, GROUP * 128)
+    ).reshape(4, 2, ROWS, GROUP * 128)
     m1, acc1 = first_part(q, own, p1, p2)
-    out = second_part(q, own, p4, p3, m1, acc1)
-    result = lax.all_to_all(
-        out.reshape(8, ROWS, GROUP * 128), group, split_axis=0, concat_axis=2, tiled=True
-    )
-    return result.reshape(ROWS, 8 * GROUP * 128)
+    core = lax.axis_index("c").astype(jnp.int32).reshape(1)
+    rest = (core, q, own, p4, p3, m1, acc1)
+    theirs = lax.ppermute(second_part(False, *rest), "c", [(0, 1), (1, 0)])
+    block = join(core, second_part(True, *rest), theirs).reshape(4, ROWS, 2 * GROUP * 128)
+    result = lax.all_to_all(block, "x", split_axis=0, concat_axis=0, tiled=True)
+    return jnp.concatenate([result[x] for x in range(4)], axis=1)
 
 
 def solution(mesh):

time: 91.1 us -> 94.8 us (1.041)
  the two profiles are of different devices: /device:TPU:1 before, /device:TPU:9 now
where the time goes in v3:
time: 94.8 us; the launch traced here: 94.3 us
  starting transfers between devices  30.7 us (32%)
  waiting for transfers between devices  27.8 us (29%)
  blocking collectives  21.5 us (23%)
  Pallas kernels  10.8 us (11%)
  local copies, waits for them, and re-layouts  2.35 us (2%)
  other arithmetic  1.04 us (1%)
    all_to_all x1, blocking collectives, body(): result = lax.all_to_all(block, 'x', split_axis=0, concat_axis=0, tiled=True)  21.5 us
    ppermute x1, waiting for transfers between devices, body(): p3 = lax.ppermute(rearrange(relay_kernel, own, p1), AXES, ring_route(2, 2))  8.2 us
    ppermute x1, waiting for transfers between devices, body(): p1 = lax.ppermute(own, AXES, ring_route(4, 0))  6.62 us
    ppermute x1, starting transfers between devices, body(): p1 = lax.ppermute(own, AXES, ring_route(4, 0))  6.58 us
    pallas_call x1, Pallas kernels, first_part(): pl.pallas_call(first_kernel, out_shape=(jax.ShapeDtypeStruct((2, GROUP *...  5.89 us
    ppermute x1, waiting for transfers between devices, body(): p4 = lax.ppermute(own, AXES, ring_route(5, 1))  5.48 us
    all_to_all x1, starting transfers between devices, body(): lax.all_to_all(packed, group, split_axis=0, concat_axis=0, tiled=True)  4.97 us
    ppermute x1, starting transfers between devices, body(): theirs = lax.ppermute(second_part(False, *rest), 'c', [(0, 1), (1, 0)])  4.8 us
  transfers between devices with their start and end apart: 7, of which 5 were waited for; matrix products, arithmetic and copies ran while one was open for 2% of the time, Pallas kernels for 9%

profile of v3, /device:TPU:9, one launch (start us, length us, event | category | flops | bytes accessed | tf_op | source)
XLA Modules:
  0.0 94.3 jit_solution(15222720419970402100)
XLA Ops:
  0.0 1.7 %shard_map.46 = bf16[8,72,256]{2,1,0:T(8,128)(2,1)} custom-call(s32[64]{0:T(128)} %pos_ref.1, bf16[64,1024]{1,0:T(8,128)(2,1)} %k_ref.1, bf16[64,1024]{1,0:T(8,128)(2,1)} %v_ref.1), custom_call_target="tpu_custom_call" | custom-call | tf_op jit(solution)/shard_map/pallas_call | solution.py:59
  1.7 5.0 %all-to-all-start.1 = ((bf16[8,72,256]{2,1,0:T(8,128)(2,1)}), bf16[8,72,256]{2,1,0:T(8,128)(2,1)S(1)}, u32[]{:S(2)}, u32[]{:S(2)}) async-start(bf16[8,72,256]{2,1,0:T(8,128)(2,1)} %shard_map.46), calls=%async_computation.1 | async-start | bytes 589824 | tf_op jit(solution)/shard_map/all_to_all | solution.py:299
  6.7 2.3 %copy.8 = bf16[8,8,8,1024]{3,2,0,1:T(8,128)(2,1)} copy(bf16[8,8,8,1024]{3,2,1,0:T(8,128)(2,1)} %bitcast.23) | data formatting | bytes 2097152 | tf_op jit(solution)/shard_map/reshape | solution.py:306
  9.0 4.5 %all-to-all-done.1.in_ref = bf16[8,72,256]{2,1,0:T(8,128)(2,1)S(1)} async-done(((bf16[8,72,256]{2,1,0:T(8,128)(2,1)}), bf16[8,72,256]{2,1,0:T(8,128)(2,1)S(1)}, u32[]{:S(2)}, u32[]{:S(2)}) %all-to-all-start.1) | async-done | bytes 294944 | tf_op jit(solution)/shard_map/all_to_all | solution.py:299
  13.5 4.5 %all-to-all-start = ((bf16[64,8,1024]{2,0,1:T(8,128)(2,1)}), bf16[64,8,1024]{2,0,1:T(8,128)(2,1)S(1)}, u32[]{:S(2)}, u32[]{:S(2)}) async-start(bf16[64,8,1024]{2,0,1:T(8,128)(2,1)} %bitcast.18), calls=%async_computation | async-start | bytes 2097152 | tf_op jit(solution)/shard_map/all_to_all | solution.py:305
  18.1 6.6 %collective-permute-start.1 = (bf16[528,256]{1,0:T(8,128)(2,1)S(1)}, bf16[528,256]{1,0:T(8,128)(2,1)S(1)}, u32[]{:S(2)}, u32[]{:S(2)}) collective-permute-start(bf16[528,256]{1,0:T(8,128)(2,1)S(1)} %shard_map.47.own_ref), channel_id=1, source_target_pairs={{256,0},{257,1},{258,2},{259,3},{260,4},{261,5},{262,6},{263,7},{2... | collective-permute-start | bytes 811016 | tf_op jit(solution)/shard_map/ppermute | solution.py:301
  24.7 2.3 %collective-permute-start.3 = (bf16[528,256]{1,0:T(8,128)(2,1)S(1)}, bf16[528,256]{1,0:T(8,128)(2,1)S(1)}, u32[]{:S(2)}, u32[]{:S(2)}) collective-permute-start(bf16[528,256]{1,0:T(8,128)(2,1)S(1)} %shard_map.47.own_ref), channel_id=1, source_target_pairs={{318,0},{319,1},{0,2},{1,3},{2,4},{3,5},{4,6},{5,7},{262,8},{263,9... | collective-permute-start | bytes 811016 | tf_op jit(solution)/shard_map/ppermute | solution.py:303
  27.0 3.6 %collective-permute-start = (bf16[528,256]{1,0:T(8,128)(2,1)S(1)}, bf16[528,256]{1,0:T(8,128)(2,1)S(1)}, u32[]{:S(2)}, u32[]{:S(2)}) collective-permute-start(bf16[528,256]{1,0:T(8,128)(2,1)S(1)} %shard_map.47.own_ref), channel_id=1, source_target_pairs={{62,0},{63,1},{256,2},{257,3},{258,4},{259,5},{260,6},{261,7},{6,8... | collective-permute-start | bytes 811016 | tf_op jit(solution)/shard_map/ppermute | solution.py:302
  30.6 6.6 %collective-permute-done.1.other_ref = bf16[528,256]{1,0:T(8,128)(2,1)S(1)} collective-permute-done((bf16[528,256]{1,0:T(8,128)(2,1)S(1)}, bf16[528,256]{1,0:T(8,128)(2,1)S(1)}, u32[]{:S(2)}, u32[]{:S(2)}) %collective-permute-start.1) | collective-permute-done | bytes 270368 | tf_op jit(solution)/shard_map/ppermute | solution.py:301
  37.3 3.8 %collective-permute-start.2 = (bf16[528,256]{1,0:T(8,128)(2,1)S(1)}, bf16[528,256]{1,0:T(8,128)(2,1)S(1)}, u32[]{:S(2)}, u32[]{:S(2)}) collective-permute-start(bf16[528,256]{1,0:T(8,128)(2,1)S(1)} %shard_map.48), channel_id=1, source_target_pairs={{316,0},{317,1},{318,2},{319,3},{0,4},{1,5},{2,6},{3,7},{260,8},{2... | collective-permute-start | bytes 811016 | tf_op jit(solution)/shard_map/ppermute | solution.py:304
  41.1 3.0 %collective-permute-done.3.p2_ref = bf16[528,256]{1,0:T(8,128)(2,1)S(1)} collective-permute-done((bf16[528,256]{1,0:T(8,128)(2,1)S(1)}, bf16[528,256]{1,0:T(8,128)(2,1)S(1)}, u32[]{:S(2)}, u32[]{:S(2)}) %collective-permute-start.3) | collective-permute-done | bytes 270368 | tf_op jit(solution)/shard_map/ppermute | solution.py:303
  44.1 0.0 all-to-all-done
  44.1 5.9 %shard_map.49 = (f32[2,2048,128]{2,1,0:T(8,128)S(1)}, f32[2,2048,256]{2,1,0:T(8,128)S(1)}) custom-call(bf16[4,2,64,1024]{3,2,1,0:T(8,128)(2,1)S(1)} %bitcast.19, bf16[528,256]{1,0:T(8,128)(2,1)S(1)} %shard_map.47.own_ref, bf16[528,256]{1,0:T(8,128)(2,1)S(1)} %collective-permute-done.1.other_ref, bf16[528,256]{1,0:T(8,128)(2,1)S(1)} %collective-permute-done.3.p2_ref), custom_call_target="tpu_custom_call" | custom-call | flops 2147483648 | bytes 8388608 | tf_op jit(solution)/shard_map/pallas_call | solution.py:261
  50.0 5.5 %collective-permute-done.p4_ref = bf16[528,256]{1,0:T(8,128)(2,1)S(1)} collective-permute-done((bf16[528,256]{1,0:T(8,128)(2,1)S(1)}, bf16[528,256]{1,0:T(8,128)(2,1)S(1)}, u32[]{:S(2)}, u32[]{:S(2)}) %collective-permute-start) | collective-permute-done | bytes 270368 | tf_op jit(solution)/shard_map/ppermute | solution.py:302
  55.5 8.2 %collective-permute-done.2.p3_ref = bf16[528,256]{1,0:T(8,128)(2,1)S(1)} collective-permute-done((bf16[528,256]{1,0:T(8,128)(2,1)S(1)}, bf16[528,256]{1,0:T(8,128)(2,1)S(1)}, u32[]{:S(2)}, u32[]{:S(2)}) %collective-permute-start.2) | collective-permute-done | bytes 270368 | tf_op jit(solution)/shard_map/ppermute | solution.py:304
  63.7 0.7 shard_map.51
  64.4 4.8 %collective-permute-start.4 = (bf16[256,1024]{1,0:T(8,128)(2,1)S(1)}, bf16[256,1024]{1,0:T(8,128)(2,1)S(1)}, u32[]{:S(2)}, u32[]{:S(2)}) collective-permute-start(bf16[256,1024]{1,0:T(8,128)(2,1)S(1)} %shard_map.51), channel_id=1, source_target_pairs={{0,1},{1,0},{2,3},{3,2},{4,5},{5,4},{6,7},{7,6},{8,9},{9,8},{10,11... | collective-permute-start | bytes 1572872 | tf_op jit(solution)/shard_map/ppermute | solution.py:311
  69.2 2.4 %shard_map.50.mine_ref = bf16[256,1024]{1,0:T(8,128)(2,1)S(1)} custom-call(s32[1]{0:T(128)} %bitcast.core_ref, bf16[4,2,64,1024]{3,2,1,0:T(8,128)(2,1)S(1)} %bitcast.21, bf16[528,256]{1,0:T(8,128)(2,1)S(1)} %shard_map.47.own_ref, bf16[528,256]{1,0:T(8,128)(2,1)S(1)} %collective-permute-done.p4_ref, bf16[528,256]{1,0:T(8,128)(2,1)S(1)} %collective-permute-done.2.p3_ref, ...), custom_call_target="tpu_custom_call" | custom-call | flops 1073741824 | bytes 8388608 | tf_op jit(solution)/shard_map/pallas_call | solution.py:279
  71.6 0.0 collective-permute-done.4.theirs_ref
  71.6 0.1 shard_map.52
  71.7 21.5 %all_to_all.25 = bf16[4,64,2048]{2,1,0:T(8,128)(2,1)S(1)} all-to-all(bf16[4,64,2048]{2,1,0:T(8,128)(2,1)S(1)} %bitcast.22), channel_id=1, replica_groups=mesh['yh'=2,'x'=4,'z'=8,'yl'=4,'c'=2] {'x'}, dimensions={0} | all-to-all | bytes 2097152 | tf_op jit(solution)/shard_map/all_to_all | solution.py:313
  93.2 0.1 slice_bitcast_fusion.3
  93.3 1.0 %pad_maximum_fusion = bf16[64,8192]{1,0:T(8,128)(2,1)} fusion(bf16[64,2048]{1,0:T(8,128)(2,1)S(1)} %get-tuple-element.10, bf16[64,2048]{1,0:T(8,128)(2,1)S(1)} %get-tuple-element.11, bf16[64,2048]{1,0:T(8,128)(2,1)S(1)} %get-tuple-element.12, bf16[64,2048]{1,0:T(8,128)(2,1)S(1)} %get-tuple-element.9), kind=kLoop, calls=%fused_computation.1 | loop fusion | flops 4194304 | bytes 2097152 | tf_op jit(solution)/shard_map/concatenate | solution.py:314
  (2 shorter events, 0.0 us)
Async XLA Ops:
  1.7 11.8 %all-to-all-start.1 = ((bf16[8,72,256]{2,1,0:T(8,128)(2,1)}), bf16[8,72,256]{2,1,0:T(8,128)(2,1)S(1)}, u32[]{:S(2)}, u32[]{:S(2)}) async-start(bf16[8,72,256]{2,1,0:T(8,128)(2,1)} %shard_map.46), calls=%async_computation.1 | async-start | bytes 589824 | tf_op jit(solution)/shard_map/all_to_all | solution.py:299
  13.5 30.6 %all-to-all-start = ((bf16[64,8,1024]{2,0,1:T(8,128)(2,1)}), bf16[64,8,1024]{2,0,1:T(8,128)(2,1)S(1)}, u32[]{:S(2)}, u32[]{:S(2)}) async-start(bf16[64,8,1024]{2,0,1:T(8,128)(2,1)} %bitcast.18), calls=%async_computation | async-start | bytes 2097152 | tf_op jit(solution)/shard_map/all_to_all | solution.py:305
  18.1 19.2 %collective-permute-start.1 = (bf16[528,256]{1,0:T(8,128)(2,1)S(1)}, bf16[528,256]{1,0:T(8,128)(2,1)S(1)}, u32[]{:S(2)}, u32[]{:S(2)}) collective-permute-start(bf16[528,256]{1,0:T(8,128)(2,1)S(1)} %shard_map.47.own_ref), channel_id=1, source_target_pairs={{256,0},{257,1},{258,2},{259,3},{260,4},{261,5},{262,6},{263,7},{2... | collective-permute-start | bytes 811016 | tf_op jit(solution)/shard_map/ppermute | solution.py:301
  24.7 19.4 %collective-permute-start.3 = (bf16[528,256]{1,0:T(8,128)(2,1)S(1)}, bf16[528,256]{1,0:T(8,128)(2,1)S(1)}, u32[]{:S(2)}, u32[]{:S(2)}) collective-permute-start(bf16[528,256]{1,0:T(8,128)(2,1)S(1)} %shard_map.47.own_ref), channel_id=1, source_target_pairs={{318,0},{319,1},{0,2},{1,3},{2,4},{3,5},{4,6},{5,7},{262,8},{263,9... | collective-permute-start | bytes 811016 | tf_op jit(solution)/shard_map/ppermute | solution.py:303
  27.0 28.5 %collective-permute-start = (bf16[528,256]{1,0:T(8,128)(2,1)S(1)}, bf16[528,256]{1,0:T(8,128)(2,1)S(1)}, u32[]{:S(2)}, u32[]{:S(2)}) collective-permute-start(bf16[528,256]{1,0:T(8,128)(2,1)S(1)} %shard_map.47.own_ref), channel_id=1, source_target_pairs={{62,0},{63,1},{256,2},{257,3},{258,4},{259,5},{260,6},{261,7},{6,8... | collective-permute-start | bytes 811016 | tf_op jit(solution)/shard_map/ppermute | solution.py:302
  37.3 26.4 %collective-permute-start.2 = (bf16[528,256]{1,0:T(8,128)(2,1)S(1)}, bf16[528,256]{1,0:T(8,128)(2,1)S(1)}, u32[]{:S(2)}, u32[]{:S(2)}) collective-permute-start(bf16[528,256]{1,0:T(8,128)(2,1)S(1)} %shard_map.48), channel_id=1, source_target_pairs={{316,0},{317,1},{318,2},{319,3},{0,4},{1,5},{2,6},{3,7},{260,8},{2... | collective-permute-start | bytes 811016 | tf_op jit(solution)/shard_map/ppermute | solution.py:304
  64.4 7.2 %collective-permute-start.4 = (bf16[256,1024]{1,0:T(8,128)(2,1)S(1)}, bf16[256,1024]{1,0:T(8,128)(2,1)S(1)}, u32[]{:S(2)}, u32[]{:S(2)}) collective-permute-start(bf16[256,1024]{1,0:T(8,128)(2,1)S(1)} %shard_map.51), channel_id=1, source_target_pairs={{0,1},{1,0},{2,3},{3,2},{4,5},{5,4},{6,7},{7,6},{8,9},{9,8},{10,11... | collective-permute-start | bytes 1572872 | tf_op jit(solution)/shard_map/ppermute | solution.py:311

commit v4 on v2

--- a/solution.py
+++ b/solution.py
@@ -64,13 +64,14 @@
     )(positions, key_tensor, value_tensor)
 
 
-def repack_kernel(in_ref, out_ref):
+def repack_kernel(in_ref, out_ref, plain_ref):
     flags = []
     for c in range(2):
         for x in range(4):
             block = in_ref[c * 4 + x]
             at = c * RUN + x * ROWS
             out_ref[at : at + ROWS, :] = block[0:ROWS, :]
+            plain_ref[at : at + ROWS, :] = block[0:ROWS, :]
         flags.append(block[ROWS : ROWS + FLAG_ROWS, 0:128])
     line = jnp.concatenate(flags, axis=1)
     out_ref[2 * RUN : 2 * RUN + 16, :] = jnp.concatenate([line, line], axis=0)
@@ -81,7 +82,8 @@
     out_ref[0:RUN, :] = own_ref[RUN : 2 * RUN, :]
     out_ref[RUN : 2 * RUN, :] = other_ref[RUN : 2 * RUN, :]
     out_ref[last, 0:128] = own_ref[last, 128:256]
-    out_ref[last, 128:256] = other_ref[last, 128:256]
+    mirror = 127.0 - own_ref[last, 128:256].astype(jnp.float32)
+    out_ref[last, 128:256] = mirror.astype(jnp.bfloat16)
 
 
 def rearrange(kernel, *operands):
@@ -92,6 +94,18 @@
         out_specs=vmem(1)[0],
         compiler_params=pltpu.CompilerParams(vmem_limit_bytes=4 * MIB),
     )(*operands)
+
+
+def repack(block):
+    return pl.pallas_call(
+        repack_kernel,
+        out_shape=tuple(
+            jax.ShapeDtypeStruct((2 * RUN + extra, 256), jnp.bfloat16) for extra in (16, 0)
+        ),
+        in_specs=vmem(1),
+        out_specs=tuple(vmem(2)),
+        compiler_params=pltpu.CompilerParams(vmem_limit_bytes=4 * MIB),
+    )(block)
 
 
 def flag(ref, half):
@@ -187,10 +201,10 @@
 
 
 def second_kernel(
-    q_ref, own_ref, p4_ref, p3_ref, m1_ref, acc1_ref, out_ref, m_ref, acc_ref, kv_ref, s_ref
+    q_ref, own_ref, p2_ref, p4_ref, p3_ref, m1_ref, acc1_ref, out_ref, m_ref, acc_ref, kv_ref, s_ref
 ):
     runs = [flag(own_ref, c) for c in range(2)]
-    near = [(p4_ref, c * RUN, flag(p4_ref, c)) for c in range(2)]
+    near = [(p4_ref, c * RUN, 127 - flag(p2_ref, c)) for c in range(2)]
     far = [(p3_ref, c * RUN, flag(p3_ref, c)) for c in range(2)]
     slots = [near + far, near]
     counts = [gather_visible(slots[i], runs[i], kv_ref, i, 0) for i in range(2)]
@@ -261,7 +275,7 @@
     return pl.pallas_call(
         second_kernel,
         out_shape=jax.ShapeDtypeStruct((2 * RUN, GROUP * 128), jnp.bfloat16),
-        in_specs=vmem(6),
+        in_specs=vmem(7),
         out_specs=vmem(1)[0],
         scratch_shapes=[
             pltpu.VMEM((2, GROUP * RUN, 128), jnp.float32),
@@ -277,18 +291,18 @@
 def body(queries, key_tensor, value_tensor, positions):
     group = ("c", "x")
     packed = pack(positions, key_tensor, value_tensor)
-    own = rearrange(
-        repack_kernel, lax.all_to_all(packed, group, split_axis=0, concat_axis=0, tiled=True)
+    own, plain = repack(
+        lax.all_to_all(packed, group, split_axis=0, concat_axis=0, tiled=True)
     )
-    p1 = lax.ppermute(own, AXES, ring_route(4, 0))
-    p4 = lax.ppermute(own, AXES, ring_route(5, 1))
+    p1 = lax.ppermute(plain, AXES, ring_route(4, 0))
+    p4 = lax.ppermute(plain, AXES, ring_route(5, 1))
     p2 = lax.ppermute(own, AXES, ring_route(1, 1))
     p3 = lax.ppermute(rearrange(relay_kernel, own, p1), AXES, ring_route(2, 2))
     q = lax.all_to_all(
         queries.reshape(ROWS, 8, GROUP * 128), group, split_axis=1, concat_axis=0, tiled=True
     ).reshape(2 * RUN, GROUP * 128)
     m1, acc1 = first_part(q, own, p1, p2)
-    out = second_part(q, own, p4, p3, m1, acc1)
+    out = second_part(q, own, p2, p4, p3, m1, acc1)
     result = lax.all_to_all(
         out.reshape(8, ROWS, GROUP * 128), group, split_axis=0, concat_axis=2, tiled=True
     )

time: 91.1 us -> 93.6 us (1.027)
  waiting for transfers between devices: 34.5 us -> 24.6 us
  blocking collectives: 19.4 us -> 26.9 us
  Pallas kernels: 8.78 us -> 14.4 us
    all_to_all x1, blocking collectives: 19.4 us -> 26.9 us  [body(): lax.all_to_all(out.reshape(8, ROWS, GROUP * 128), group, split_axis=0, co...]
    ppermute x2, waiting for transfers between devices: 20.9 us -> 13.7 us  [the longest x1 13.7 us: body(): p1 = lax.ppermute(plain, AXES, ring_route(4, 0))]
    pallas_call x1, Pallas kernels: 2.15 us -> 8.69 us  [first_part(): pl.pallas_call(first_kernel, out_shape=(jax.ShapeDtypeStruct((2, GROUP *...]
    ppermute x1, waiting for transfers between devices: 8.94 us -> 6.26 us  [body(): p2 = lax.ppermute(own, AXES, ring_route(1, 1))]
    pallas_call x1, Pallas kernels: 4.86 us -> 3.92 us  [second_part(): pl.pallas_call(second_kernel, out_shape=jax.ShapeDtypeStruct((2 * RUN, GR...]
  transfers between devices with their start and end apart: 6 -> 6, of which waited for: 4 -> 3; matrix products, arithmetic and copies ran while one was open for 3% -> 2% of each run, Pallas kernels for 2% -> 9%
where the time goes in v4:
time: 93.6 us; the launch traced here: 93.1 us
  blocking collectives  26.9 us (29%)
  waiting for transfers between devices  24.6 us (26%)
  starting transfers between devices  23.8 us (25%)
  Pallas kernels  14.4 us (15%)
  local copies, waits for them, and re-layouts  3.35 us (4%)
    all_to_all x1, blocking collectives, body(): lax.all_to_all(out.reshape(8, ROWS, GROUP * 128), group, split_axis=0, co...  26.9 us
    ppermute x1, waiting for transfers between devices, body(): p1 = lax.ppermute(plain, AXES, ring_route(4, 0))  13.7 us
    all_to_all x1, starting transfers between devices, body(): lax.all_to_all(packed, group, split_axis=0, concat_axis=0, tiled=True)  10.2 us
    pallas_call x1, Pallas kernels, first_part(): pl.pallas_call(first_kernel, out_shape=(jax.ShapeDtypeStruct((2, GROUP *...  8.69 us
    ppermute x1, waiting for transfers between devices, body(): p2 = lax.ppermute(own, AXES, ring_route(1, 1))  6.26 us
    all_to_all x1, waiting for transfers between devices, body(): lax.all_to_all(packed, group, split_axis=0, concat_axis=0, tiled=True)  4.63 us
    pallas_call x1, Pallas kernels, second_part(): pl.pallas_call(second_kernel, out_shape=jax.ShapeDtypeStruct((2 * RUN, GR...  3.92 us
    all_to_all x1, starting transfers between devices, body(): lax.all_to_all(queries.reshape(ROWS, 8, GROUP * 128), group, split_axis=1...  3.85 us
  transfers between devices with their start and end apart: 6, of which 3 were waited for; matrix products, arithmetic and copies ran while one was open for 2% of the time, Pallas kernels for 9%

profile of v4, /device:TPU:1, one launch (start us, length us, event | category | flops | bytes accessed | tf_op | source)
XLA Modules:
  0.0 93.1 jit_solution(1450342473979721844)
XLA Ops:
  0.0 1.7 %shard_map.46 = bf16[8,72,256]{2,1,0:T(8,128)(2,1)} custom-call(s32[64]{0:T(128)} %pos_ref.1, bf16[64,1024]{1,0:T(8,128)(2,1)} %k_ref.1, bf16[64,1024]{1,0:T(8,128)(2,1)} %v_ref.1), custom_call_target="tpu_custom_call" | custom-call | tf_op jit(solution)/shard_map/pallas_call | solution.py:58
  1.7 10.2 %all-to-all-start.1 = ((bf16[8,72,256]{2,1,0:T(8,128)(2,1)}), bf16[8,72,256]{2,1,0:T(8,128)(2,1)S(1)}, u32[]{:S(2)}, u32[]{:S(2)}) async-start(bf16[8,72,256]{2,1,0:T(8,128)(2,1)} %shard_map.46), calls=%async_computation.1 | async-start | bytes 589824 | tf_op jit(solution)/shard_map/all_to_all | solution.py:295
  11.9 2.3 %copy.11 = bf16[8,8,8,1024]{3,2,0,1:T(8,128)(2,1)} copy(bf16[8,8,8,1024]{3,2,1,0:T(8,128)(2,1)} %bitcast.22) | data formatting | bytes 2097152 | tf_op jit(solution)/shard_map/reshape | solution.py:302
  14.2 4.6 %all-to-all-done.1.in_ref = bf16[8,72,256]{2,1,0:T(8,128)(2,1)S(1)} async-done(((bf16[8,72,256]{2,1,0:T(8,128)(2,1)}), bf16[8,72,256]{2,1,0:T(8,128)(2,1)S(1)}, u32[]{:S(2)}, u32[]{:S(2)}) %all-to-all-start.1) | async-done | bytes 294944 | tf_op jit(solution)/shard_map/all_to_all | solution.py:295
  18.9 3.8 %all-to-all-start = ((bf16[64,8,1024]{2,0,1:T(8,128)(2,1)}), bf16[64,8,1024]{2,0,1:T(8,128)(2,1)S(1)}, u32[]{:S(2)}, u32[]{:S(2)}) async-start(bf16[64,8,1024]{2,0,1:T(8,128)(2,1)} %bitcast.17), calls=%async_computation | async-start | bytes 2097152 | tf_op jit(solution)/shard_map/all_to_all | solution.py:301
  22.8 3.0 %collective-permute-start.2 = (bf16[512,256]{1,0:T(8,128)(2,1)S(1)}, bf16[512,256]{1,0:T(8,128)(2,1)S(1)}, u32[]{:S(2)}, u32[]{:S(2)}) collective-permute-start(bf16[512,256]{1,0:T(8,128)(2,1)S(1)} %get-tuple-element.10), channel_id=1, source_target_pairs={{256,0},{257,1},{258,2},{259,3},{260,4},{261,5},{262,6},{263,7},{2... | collective-permute-start | bytes 786440 | tf_op jit(solution)/shard_map/ppermute | solution.py:297
  25.8 2.3 %collective-permute-start = (bf16[528,256]{1,0:T(8,128)(2,1)S(1)}, bf16[528,256]{1,0:T(8,128)(2,1)S(1)}, u32[]{:S(2)}, u32[]{:S(2)}) collective-permute-start(bf16[528,256]{1,0:T(8,128)(2,1)S(1)} %get-tuple-element.9.own_ref), channel_id=1, source_target_pairs={{318,0},{319,1},{0,2},{1,3},{2,4},{3,5},{4,6},{5,7},{262,8},{263,9... | collective-permute-start | bytes 811016 | tf_op jit(solution)/shard_map/ppermute | solution.py:299
  28.1 13.7 %collective-permute-done.2.other_ref = bf16[512,256]{1,0:T(8,128)(2,1)S(1)} collective-permute-done((bf16[512,256]{1,0:T(8,128)(2,1)S(1)}, bf16[512,256]{1,0:T(8,128)(2,1)S(1)}, u32[]{:S(2)}, u32[]{:S(2)}) %collective-permute-start.2) | collective-permute-done | bytes 262176 | tf_op jit(solution)/shard_map/ppermute | solution.py:297
  41.8 1.9 %collective-permute-start.3 = (bf16[528,256]{1,0:T(8,128)(2,1)S(1)}, bf16[528,256]{1,0:T(8,128)(2,1)S(1)}, u32[]{:S(2)}, u32[]{:S(2)}) collective-permute-start(bf16[528,256]{1,0:T(8,128)(2,1)S(1)} %shard_map.48), channel_id=1, source_target_pairs={{316,0},{317,1},{318,2},{319,3},{0,4},{1,5},{2,6},{3,7},{260,8},{2... | collective-permute-start | bytes 811016 | tf_op jit(solution)/shard_map/ppermute | solution.py:300
  43.7 2.5 %collective-permute-start.1 = (bf16[512,256]{1,0:T(8,128)(2,1)S(1)}, bf16[512,256]{1,0:T(8,128)(2,1)S(1)}, u32[]{:S(2)}, u32[]{:S(2)}) collective-permute-start(bf16[512,256]{1,0:T(8,128)(2,1)S(1)} %get-tuple-element.10), channel_id=1, source_target_pairs={{62,0},{63,1},{256,2},{257,3},{258,4},{259,5},{260,6},{261,7},{6,8... | collective-permute-start | bytes 786440 | tf_op jit(solution)/shard_map/ppermute | solution.py:298
  46.2 6.3 %collective-permute-done.p2_ref = bf16[528,256]{1,0:T(8,128)(2,1)S(1)} collective-permute-done((bf16[528,256]{1,0:T(8,128)(2,1)S(1)}, bf16[528,256]{1,0:T(8,128)(2,1)S(1)}, u32[]{:S(2)}, u32[]{:S(2)}) %collective-permute-start) | collective-permute-done | bytes 270368 | tf_op jit(solution)/shard_map/ppermute | solution.py:299
  52.5 0.0 all-to-all-done
  52.5 8.7 %shard_map.49 = (f32[2,2048,128]{2,1,0:T(8,128)S(1)}, f32[2,2048,256]{2,1,0:T(8,128)S(1)}) custom-call(bf16[512,1024]{1,0:T(8,128)(2,1)S(1)} %bitcast.18, bf16[528,256]{1,0:T(8,128)(2,1)S(1)} %get-tuple-element.9.own_ref, bf16[512,256]{1,0:T(8,128)(2,1)S(1)} %collective-permute-done.2.other_ref, bf16[528,256]{1,0:T(8,128)(2,1)S(1)} %collective-permute-done.p2_ref), custom_call_target="tpu_custom_call" | custom-call | flops 2147483648 | bytes 8388608 | tf_op jit(solution)/shard_map/pallas_call | solution.py:257
  61.2 0.0 collective-permute-done.1.p4_ref
  61.2 0.0 collective-permute-done.3.p3_ref
  61.2 3.9 %shard_map.50 = bf16[512,1024]{1,0:T(8,128)(2,1)S(1)} custom-call(bf16[512,1024]{1,0:T(8,128)(2,1)S(1)} %bitcast.19, bf16[528,256]{1,0:T(8,128)(2,1)S(1)} %get-tuple-element.9.own_ref, bf16[528,256]{1,0:T(8,128)(2,1)S(1)} %collective-permute-done.p2_ref, bf16[512,256]{1,0:T(8,128)(2,1)S(1)} %collective-permute-done.1.p4_ref, ...), custom_call_target="tpu_custom_call" | custom-call | flops 2147483648 | bytes 8388608 | tf_op jit(solution)/shard_map/pallas_call | solution.py:275
  65.1 26.9 %all_to_all.35 = bf16[8,64,1024]{2,1,0:T(8,128)(2,1)S(1)} all-to-all(bf16[8,64,1024]{2,1,0:T(8,128)(2,1)S(1)} %bitcast.20), channel_id=1, replica_groups=mesh['yh'=2,'x'=4,'z'=8,'yl'=4,'c'=2] {'c','x'}, dimensions={0} | all-to-all | bytes 2097152 | tf_op jit(solution)/shard_map/all_to_all | solution.py:306
  92.1 1.1 %copy.8 = bf16[8,8,8,1024]{3,1,2,0:T(8,128)(2,1)} copy(bf16[8,8,8,1024]{3,1,0,2:T(8,128)(2,1)S(1)} %bitcast.21) | data formatting | bytes 2097152
  (2 shorter events, 0.1 us)
Async XLA Ops:
  1.7 17.1 %all-to-all-start.1 = ((bf16[8,72,256]{2,1,0:T(8,128)(2,1)}), bf16[8,72,256]{2,1,0:T(8,128)(2,1)S(1)}, u32[]{:S(2)}, u32[]{:S(2)}) async-start(bf16[8,72,256]{2,1,0:T(8,128)(2,1)} %shard_map.46), calls=%async_computation.1 | async-start | bytes 589824 | tf_op jit(solution)/shard_map/all_to_all | solution.py:295
  18.9 33.6 %all-to-all-start = ((bf16[64,8,1024]{2,0,1:T(8,128)(2,1)}), bf16[64,8,1024]{2,0,1:T(8,128)(2,1)S(1)}, u32[]{:S(2)}, u32[]{:S(2)}) async-start(bf16[64,8,1024]{2,0,1:T(8,128)(2,1)} %bitcast.17), calls=%async_computation | async-start | bytes 2097152 | tf_op jit(solution)/shard_map/all_to_all | solution.py:301
  22.8 19.0 %collective-permute-start.2 = (bf16[512,256]{1,0:T(8,128)(2,1)S(1)}, bf16[512,256]{1,0:T(8,128)(2,1)S(1)}, u32[]{:S(2)}, u32[]{:S(2)}) collective-permute-start(bf16[512,256]{1,0:T(8,128)(2,1)S(1)} %get-tuple-element.10), channel_id=1, source_target_pairs={{256,0},{257,1},{258,2},{259,3},{260,4},{261,5},{262,6},{263,7},{2... | collective-permute-start | bytes 786440 | tf_op jit(solution)/shard_map/ppermute | solution.py:297
  25.8 26.7 %collective-permute-start = (bf16[528,256]{1,0:T(8,128)(2,1)S(1)}, bf16[528,256]{1,0:T(8,128)(2,1)S(1)}, u32[]{:S(2)}, u32[]{:S(2)}) collective-permute-start(bf16[528,256]{1,0:T(8,128)(2,1)S(1)} %get-tuple-element.9.own_ref), channel_id=1, source_target_pairs={{318,0},{319,1},{0,2},{1,3},{2,4},{3,5},{4,6},{5,7},{262,8},{263,9... | collective-permute-start | bytes 811016 | tf_op jit(solution)/shard_map/ppermute | solution.py:299
  41.8 19.4 %collective-permute-start.3 = (bf16[528,256]{1,0:T(8,128)(2,1)S(1)}, bf16[528,256]{1,0:T(8,128)(2,1)S(1)}, u32[]{:S(2)}, u32[]{:S(2)}) collective-permute-start(bf16[528,256]{1,0:T(8,128)(2,1)S(1)} %shard_map.48), channel_id=1, source_target_pairs={{316,0},{317,1},{318,2},{319,3},{0,4},{1,5},{2,6},{3,7},{260,8},{2... | collective-permute-start | bytes 811016 | tf_op jit(solution)/shard_map/ppermute | solution.py:300
  43.7 17.4 %collective-permute-start.1 = (bf16[512,256]{1,0:T(8,128)(2,1)S(1)}, bf16[512,256]{1,0:T(8,128)(2,1)S(1)}, u32[]{:S(2)}, u32[]{:S(2)}) collective-permute-start(bf16[512,256]{1,0:T(8,128)(2,1)S(1)} %get-tuple-element.10), channel_id=1, source_target_pairs={{62,0},{63,1},{256,2},{257,3},{258,4},{259,5},{260,6},{261,7},{6,8... | collective-permute-start | bytes 786440 | tf_op jit(solution)/shard_map/ppermute | solution.py:298
